TPU v7x, 32 devices: a whole 2x2x4 slice. The times are simulated.
32 devices in a mesh: stream: 2 (over core), dp: 16 (over z, y, x).
Axes of the slice: x: 2, y: 2, z: 4, core: 2. Of those that a mesh axis runs over, the one named last changes fastest.
Arguments:
- x_in: bfloat16 [2, 64, 128, 768], P('stream', 'dp'), may hold values from -6 to 6
- lengths: int32 [64], P('dp'), may hold values from 33 to 100, as said below
- drops: int32 [64], P('dp'), may hold values 0 or 1
- proj_master: float32 [2, 2, 3, 768, 768], P('stream', None, None, 'dp'), may hold values from -0.21875 to 0.21875
- out_master: float32 [2, 2, 768, 768], P('stream', None, 'dp'), may hold values from -1.25 to 1.25
- ffn_in_master: float32 [2, 768, 3072], P('stream', 'dp'), may hold values from -0.21875 to 0.21875
- ffn_out_master: float32 [2, 3072, 768], P('stream', 'dp'), may hold values from -0.109375 to 0.109375
- join_master: float32 [2, 2, 768, 768], P('stream', None, 'dp'), may hold values from -0.21875 to 0.21875
- vectors: float32 [2, 7, 768], P('stream', None, 'dp'), may hold values from -2 to 2.2
- cotangent: bfloat16 [2, 64, 128, 768], P('stream', 'dp'), may hold values from -6 to 6
Outputs:
- joined: bfloat16 [2, 64, 128, 768], P('stream', 'dp')
- x_grad: bfloat16 [2, 64, 128, 768], P('stream', 'dp')
- proj_grad: float32 [2, 2, 3, 768, 768], P('stream', None, None, 'dp')
- out_grad: float32 [2, 2, 768, 768], P('stream', None, 'dp')
- ffn_in_grad: float32 [2, 768, 3072], P('stream', 'dp')
- ffn_out_grad: float32 [2, 3072, 768], P('stream', 'dp')
- join_grad: float32 [2, 2, 768, 768], P('stream', None, 'dp')
- vectors_grad: float32 [2, 7, 768], P('stream', None, 'dp')
Inputs may be any that keep to these rules, and one draw needn't show every extreme that they name: `lengths`: each page holds 33 to 100 regions; some page holds exactly 100.
All inputs are finite; a program needn't handle non-finite values. No bound on the sum of `drops` on one device may be relied on, other than what follows from the above.
Results may differ from a plain program's by a relative error of at most 0.023.
Values may be sent and summed in bfloat16 or wider, within the bound.
A program may use at most 256 MiB of HBM per device.

v0:
```python
from functools import partial

import jax
import jax.numpy as jnp
from jax import lax
from jax.sharding import PartitionSpec as P

HEADS = 12


EPSILON = 1e-05


def swapped(array, axis, stride):
    return lax.ppermute(array, axis, [(i, i ^ 1 << stride) for i in range(lax.axis_size(axis))])


def product(left, right):
    return jnp.dot(left, right, preferred_element_type=jnp.float32)


def outer_sum(left, right):
    return lax.dot_general(
        left, right, (((0,), (0,)), ((), ())), preferred_element_type=jnp.float32
    )


def times_transposed(left, right):
    return lax.dot_general(
        left, right, (((1,), (1,)), ((), ())), preferred_element_type=jnp.float32
    )


def norm_forward(values, gain, shift):
    centre = values - jnp.mean(values, axis=-1, keepdims=True)
    inverse = lax.rsqrt(jnp.mean(centre * centre, axis=-1, keepdims=True) + EPSILON)
    unit = centre * inverse
    return (unit * gain + shift, unit, inverse)


def norm_backward(grad, unit, inverse, gain):
    scaled = grad * gain
    inner = (
        scaled
        - jnp.mean(scaled, axis=-1, keepdims=True)
        - unit * jnp.mean(scaled * unit, axis=-1, keepdims=True)
    )
    return (inverse * inner, jnp.sum(grad * unit, axis=0), jnp.sum(grad, axis=0))


def heads_view(values, pages):
    return values.reshape(pages, values.shape[0] // pages, HEADS, values.shape[1] // HEADS)


def masked_scores(query, keys, key_mask, pages):
    scale = (query.shape[1] // HEADS) ** (-0.5)
    scores = (
        jnp.einsum(
            "pqhe,pkhe->phqk",
            heads_view(query, pages),
            heads_view(keys, pages),
            preferred_element_type=jnp.float32,
        )
        * scale
    )
    return jnp.where(key_mask[:, None, None, :], scores, -1e30)


def attend_forward(query, keys, values, key_mask, pages):
    scores = masked_scores(query, keys, key_mask, pages)
    top = jnp.max(scores, axis=-1, keepdims=True)
    weights = jnp.exp(scores - top)
    total = jnp.sum(weights, axis=-1, keepdims=True)
    probs = (weights / total).astype(jnp.bfloat16)
    mixed = jnp.einsum(
        "phqk,pkhe->pqhe", probs, heads_view(values, pages), preferred_element_type=jnp.float32
    )
    return (mixed.reshape(query.shape).astype(jnp.bfloat16), top + jnp.log(total))


def attend_backward(grad_out, query, keys, values, key_mask, logsum, pages):
    scale = (query.shape[1] // HEADS) ** (-0.5)
    probs = jnp.exp(masked_scores(query, keys, key_mask, pages) - logsum)
    grad_heads = heads_view(grad_out, pages)
    grad_probs = jnp.einsum(
        "pqhe,pkhe->phqk", grad_heads, heads_view(values, pages), preferred_element_type=jnp.float32
    )
    grad_scores = (
        probs * (grad_probs - jnp.sum(grad_probs * probs, axis=-1, keepdims=True))
    ).astype(jnp.bfloat16)
    grad_query = (
        jnp.einsum(
            "phqk,pkhe->pqhe",
            grad_scores,
            heads_view(keys, pages),
            preferred_element_type=jnp.float32,
        )
        * scale
    )
    grad_keys = (
        jnp.einsum(
            "phqk,pqhe->pkhe",
            grad_scores,
            heads_view(query, pages),
            preferred_element_type=jnp.float32,
        )
        * scale
    )
    grad_values = jnp.einsum(
        "phqk,pqhe->pkhe",
        probs.astype(jnp.bfloat16),
        grad_heads,
        preferred_element_type=jnp.float32,
    )
    shape = query.shape
    return (
        grad_query.reshape(shape).astype(jnp.bfloat16),
        grad_keys.reshape(shape).astype(jnp.bfloat16),
        grad_values.reshape(shape).astype(jnp.bfloat16),
    )


def local(
    x_in,
    lengths,
    drops,
    proj_master,
    out_master,
    ffn_in_master,
    ffn_out_master,
    join_master,
    vectors,
    cotangent,
):
    pages = x_in.shape[1]
    slots = x_in.shape[2]
    width = x_in.shape[3]
    rows = pages * slots
    gathered = (
        lax.all_gather(proj_master.astype(jnp.bfloat16), "dp", axis=3, tiled=True),
        lax.all_gather(out_master.astype(jnp.bfloat16), "dp", axis=2, tiled=True),
        lax.all_gather(ffn_in_master.astype(jnp.bfloat16), "dp", axis=1, tiled=True),
        lax.all_gather(ffn_out_master.astype(jnp.bfloat16), "dp", axis=1, tiled=True),
        lax.all_gather(join_master.astype(jnp.bfloat16), "dp", axis=2, tiled=True),
        lax.all_gather(vectors.astype(jnp.bfloat16), "dp", axis=2, tiled=True),
    )
    proj_w = gathered[0][0]
    out_w = gathered[1][0]
    ffin_w = gathered[2][0]
    ffout_w = gathered[3][0]
    join_w = gathered[4][0]
    vec_w = gathered[5][0].astype(jnp.float32)
    key_mask = jnp.arange(slots, dtype=jnp.int32)[None, :] < lengths[:, None]
    row_mask = key_mask.reshape(rows, 1).astype(jnp.float32)
    keep = (1 - drops).astype(jnp.float32)
    keep_rows = jnp.broadcast_to(keep[:, None], (pages, slots)).reshape(rows, 1)
    source = x_in[0].reshape(rows, width)
    own_keys = product(source, proj_w[0, 1]).astype(jnp.bfloat16)
    own_values = product(source, proj_w[0, 2]).astype(jnp.bfloat16)
    far_keys, far_values = swapped((own_keys, own_values), "stream", 0)
    cross_query = product(source, proj_w[0, 0]).astype(jnp.bfloat16)
    cross_out, cross_logsum = attend_forward(cross_query, far_keys, far_values, key_mask, pages)
    first, unit_one, inverse_one = norm_forward(
        source.astype(jnp.float32) + product(cross_out, out_w[0]) * keep_rows, vec_w[0], vec_w[1]
    )
    first_low = first.astype(jnp.bfloat16)
    self_query = product(first_low, proj_w[1, 0]).astype(jnp.bfloat16)
    self_keys = product(first_low, proj_w[1, 1]).astype(jnp.bfloat16)
    self_values = product(first_low, proj_w[1, 2]).astype(jnp.bfloat16)
    self_out, self_logsum = attend_forward(self_query, self_keys, self_values, key_mask, pages)
    second, unit_two, inverse_two = norm_forward(
        first + product(self_out, out_w[1]), vec_w[2], vec_w[3]
    )
    second_low = second.astype(jnp.bfloat16)
    hidden = product(second_low, ffin_w)
    gelu_exact = partial(jax.nn.gelu, approximate=False)
    active_f32, gelu_pull = jax.vjp(gelu_exact, hidden)
    active = active_f32.astype(jnp.bfloat16)
    third, unit_three, inverse_three = norm_forward(
        second + product(active, ffout_w), vec_w[4], vec_w[5]
    )
    state = third.astype(jnp.bfloat16)
    far_state = swapped(state, "stream", 0)
    state_f32 = state.astype(jnp.float32)
    far_f32 = far_state.astype(jnp.float32)
    gate = jax.nn.sigmoid(product(state, join_w[0]) + product(far_state, join_w[1]) + vec_w[6])
    joined = ((gate * state_f32 + (1.0 - gate) * far_f32) * row_mask).astype(jnp.bfloat16)
    grad_joined = cotangent[0].reshape(rows, width).astype(jnp.float32) * row_mask
    grad_logits = (grad_joined * (state_f32 - far_f32) * gate * (1.0 - gate)).astype(jnp.bfloat16)
    grad_join = jnp.stack([outer_sum(state, grad_logits), outer_sum(far_state, grad_logits)])
    grad_bias = jnp.sum(grad_logits.astype(jnp.float32), axis=0)
    grad_far = (grad_joined * (1.0 - gate) + times_transposed(grad_logits, join_w[1])).astype(
        jnp.bfloat16
    )
    returned = swapped(grad_far, "stream", 0)
    grad_third = (
        grad_joined * gate + times_transposed(grad_logits, join_w[0]) + returned.astype(jnp.float32)
    )
    grad_res3, gain_three, shift_three = norm_backward(
        grad_third, unit_three, inverse_three, vec_w[4]
    )
    grad_res3_low = grad_res3.astype(jnp.bfloat16)
    grad_ffout = outer_sum(active, grad_res3_low)
    grad_hidden = gelu_pull(times_transposed(grad_res3_low, ffout_w))[0].astype(jnp.bfloat16)
    grad_ffin = outer_sum(second_low, grad_hidden)
    grad_second = grad_res3 + times_transposed(grad_hidden, ffin_w)
    grad_res2, gain_two, shift_two = norm_backward(grad_second, unit_two, inverse_two, vec_w[2])
    grad_res2_low = grad_res2.astype(jnp.bfloat16)
    grad_out_self = outer_sum(self_out, grad_res2_low)
    grad_self_out = times_transposed(grad_res2_low, out_w[1]).astype(jnp.bfloat16)
    grad_q2, grad_k2, grad_v2 = attend_backward(
        grad_self_out, self_query, self_keys, self_values, key_mask, self_logsum, pages
    )
    grad_proj_self = jnp.stack(
        [
            outer_sum(first_low, grad_q2),
            outer_sum(first_low, grad_k2),
            outer_sum(first_low, grad_v2),
        ]
    )
    grad_first = (
        grad_res2
        + times_transposed(grad_q2, proj_w[1, 0])
        + times_transposed(grad_k2, proj_w[1, 1])
        + times_transposed(grad_v2, proj_w[1, 2])
    )
    grad_res1, gain_one, shift_one = norm_backward(grad_first, unit_one, inverse_one, vec_w[0])
    grad_branch = (grad_res1 * keep_rows).astype(jnp.bfloat16)
    grad_out_cross = outer_sum(cross_out, grad_branch)
    grad_cross_out = times_transposed(grad_branch, out_w[0]).astype(jnp.bfloat16)
    grad_q1, grad_far_keys, grad_far_values = attend_backward(
        grad_cross_out, cross_query, far_keys, far_values, key_mask, cross_logsum, pages
    )
    back_keys, back_values = swapped((grad_far_keys, grad_far_values), "stream", 0)
    grad_proj_cross = jnp.stack(
        [outer_sum(source, grad_q1), outer_sum(source, back_keys), outer_sum(source, back_values)]
    )
    grad_source = (
        grad_res1
        + times_transposed(grad_q1, proj_w[0, 0])
        + times_transposed(back_keys, proj_w[0, 1])
        + times_transposed(back_values, proj_w[0, 2])
    )
    grad_proj = jnp.stack([grad_proj_cross, grad_proj_self])[None]
    grad_out = jnp.stack([grad_out_cross, grad_out_self])[None]
    grad_vectors = jnp.stack(
        [gain_one, shift_one, gain_two, shift_two, gain_three, shift_three, grad_bias]
    )[None]
    all_sums = (
        lax.psum_scatter(grad_proj, "dp", scatter_dimension=3, tiled=True),
        lax.psum_scatter(grad_out, "dp", scatter_dimension=2, tiled=True),
        lax.psum_scatter(grad_ffin[None], "dp", scatter_dimension=1, tiled=True),
        lax.psum_scatter(grad_ffout[None], "dp", scatter_dimension=1, tiled=True),
        lax.psum_scatter(grad_join[None], "dp", scatter_dimension=2, tiled=True),
        lax.psum_scatter(grad_vectors, "dp", scatter_dimension=2, tiled=True),
    )
    proj_part, out_part, ffin_part, ffout_part, join_part, vectors_part = all_sums
    joined_out = joined.reshape(1, pages, slots, width)
    x_grad = grad_source.astype(jnp.bfloat16).reshape(1, pages, slots, width)
    return (joined_out, x_grad, proj_part, out_part, ffin_part, ffout_part, join_part, vectors_part)


def solution(mesh):
    placed = (
        P("stream", "dp", None, None),
        P("dp"),
        P("dp"),
        P("stream", None, None, "dp", None),
        P("stream", None, "dp", None),
        P("stream", "dp", None),
        P("stream", "dp", None),
        P("stream", None, "dp", None),
        P("stream", None, "dp"),
        P("stream", "dp", None, None),
    )
    return jax.shard_map(
        local,
        mesh=mesh,
        in_specs=placed,
        out_specs=(
            P("stream", "dp", None, None),
            P("stream", "dp", None, None),
            P("stream", None, None, "dp", None),
            P("stream", None, "dp", None),
            P("stream", "dp", None),
            P("stream", "dp", None),
            P("stream", None, "dp", None),
            P("stream", None, "dp"),
        ),
        check_vma=False,
    )
```

profile of v0, /device:TPU:0, one launch (start us, length us, event | category | flops | bytes accessed | tf_op | source)
XLA Modules:
  0.0 1656.6 jit_solution(9890040917740383671)
XLA Ops:
  7.2 2.1 convert_element_type.219
  12.7 102.7 %all-gather.6.cloned.1.call-done = bf16[1,2,3,768,768]{4,3,2,1,0:T(8,128)(2,1)} async-done(((bf16[1,2,3,48,768]{4,3,2,1,0:T(8,128)(2,1)}), bf16[1,2,3,768,768]{4,3,2,1,0:T(8,128)(2,1)}) %all-gather.6.cloned.1.call-update) | async-done | bytes 7077904 | tf_op jit(solution)/shard_map/all_gather | solution.py:140
  115.4 2.9 convolution_convert_fusion.5
  118.3 3.0 convolution_convert_fusion.7
  122.0 41.3 %all_gather.20 = bf16[1,7,768]{1,0,2:T(2,128)(2,1)S(1)} all-gather(bf16[1,7,48]{1,0,2:T(2,128)(2,1)S(1)} %copy.191), channel_id=1, replica_groups=mesh['stream'=2,'dp'=16] {'dp'}, dimensions={2}, use_global_device_ids=true | all-gather | bytes 11424 | tf_op jit(solution)/shard_map/all_gather | solution.py:145
  163.6 16.7 %slice_reduce_fusion = (f32[768]{0:T(1024)S(1)}, f32[768]{0:T(1024)S(1)}, f32[768]{0:T(1024)S(1)}, f32[768]{0:T(1024)S(1)}, f32[768]{0:T(1024)S(1)}, /*index=5*/f32[768]{0:T(1024)S(1)}, f32[768]{0:T(1024)S(1)}) fusion(f32[1,7,768]{1,0,2:T(1,128)S(1)} %convert_element_type.230), kind=kLoop, calls=%fused_computation.198 | loop fusion | bytes 43008 | tf_op jit(solution)/shard_map/slice | solution.py:186
  180.3 2.0 convolution_convert_fusion.6
  186.5 2.4 fusion.125
  192.2 2.7 fusion.126
  196.0 3.2 convolution_convert_fusion.2
  199.3 2.9 convolution_convert_fusion.3
  202.2 3.0 convolution_convert_fusion.4
  205.2 2.3 copy.194
  207.5 2.4 reshape.228
  209.9 2.3 copy.193
  212.2 2.4 reshape.227
  214.7 2.3 copy.192
  217.0 2.6 reshape.226
  219.6 2.4 fusion.127
  228.6 34.4 %all-gather.10.cloned.1.call-done = bf16[1,768,3072]{2,1,0:T(8,128)(2,1)} async-done(((bf16[1,48,3072]{2,1,0:T(8,128)(2,1)}), bf16[1,768,3072]{2,1,0:T(8,128)(2,1)}) %all-gather.10.cloned.1.call-update) | async-done | bytes 4718608 | tf_op jit(solution)/shard_map/all_gather | solution.py:142
  263.0 21.0 %multiply_convert_fusion = (bf16[512,3072]{1,0:T(8,128)(2,1)}, f32[512,3072]{1,0:T(8,128)}, f32[512,3072]{1,0:T(8,128)}) fusion(bf16[1,768,3072]{2,1,0:T(8,128)(2,1)} %all-gather.10.cloned.1.call-done, f32[512,768]{1,0:T(8,128)} %copy-done.23, f32[768]{0:T(1024)S(1)} %get-tuple-element.63, f32[768]{0:T(1024)S(1)} %get-tuple-element.64, ...), kind=kOutput, calls=%fused_computation.6 | convolution fusion | flops 2520121344 | bytes 22030336 | tf_op jit(solution)/shard_map/dot_general | solution.py:19
  284.0 61.3 %all-gather.12.cloned.1.call-done = bf16[1,3072,768]{2,1,0:T(8,128)(2,1)} async-done(((bf16[1,192,768]{2,1,0:T(8,128)(2,1)}), bf16[1,3072,768]{2,1,0:T(8,128)(2,1)}) %all-gather.12.cloned.1.call-update) | async-done | bytes 4718608 | tf_op jit(solution)/shard_map/all_gather | solution.py:143
  345.3 6.4 fusion.129
  353.3 55.6 %all-gather.14.cloned.1.call-done = bf16[1,2,768,768]{3,2,1,0:T(8,128)(2,1)} async-done(((bf16[1,2,48,768]{3,2,1,0:T(8,128)(2,1)}), bf16[1,2,768,768]{3,2,1,0:T(8,128)(2,1)}) %all-gather.14.cloned.1.call-update) | async-done | bytes 2359312 | tf_op jit(solution)/shard_map/all_gather | solution.py:144
  408.9 2.4 fusion.74
  411.3 4.1 convert_reduce_fusion
  416.5 2.2 collective-permute-done.3
  420.8 9.2 add_convert_fusion
  430.1 5.1 multiply_reduce_fusion.3
  437.3 1.7 convolution_convert_fusion.1
  439.1 2.3 copy.200
  441.4 2.6 reshape.230
  444.0 3.5 fusion.62
  453.4 2.2 convolution_bitcast_fusion.3
  457.8 2.2 convolution_bitcast_fusion.2
  463.9 1.7 convolution_convert_fusion
  465.6 2.3 copy.212
  467.9 2.6 reshape.231
  470.5 3.3 fusion.59
  480.5 2.1 convolution_bitcast_fusion.4
  487.7 2.8 copy.217
  490.8 2.1 convolution_bitcast_fusion.11
  492.9 5.0 maximum_bitcast_fusion.2
  497.9 1.9 convolution_bitcast_fusion.10
  499.8 1.9 convolution_bitcast_fusion.9
  501.7 3.4 maximum_bitcast_fusion.1
  505.1 12.0 maximum_bitcast_fusion
  517.1 21.7 %copy.227 = f32[1,2,3,768,768]{4,1,2,0,3:T(2,128)} copy(f32[1,2,3,768,768]{3,4,2,1,0:T(8,128)} %maximum_bitcast_fusion) | data formatting | bytes 28311552 | tf_op jit(solution)/shard_map/broadcast_in_dim | solution.py:244
  540.0 1.9 convolution_bitcast_fusion.6
  541.9 1.9 convolution_bitcast_fusion.5
  543.9 2.5 maximum_bitcast_fusion.4
  547.7 2.0 convolution_bitcast_fusion.7
  550.6 2.5 maximum_bitcast_fusion.3
  554.5 7.2 convolution_bitcast_fusion.1
  563.2 8.2 convolution_bitcast_fusion
  573.2 3.3 fusion.70
  576.5 34.6 %reduce-scatter.16.cloned.1.call-done = f32[48,7]{1,0:T(8,128)} async-done(((f32[768,7]{1,0:T(8,128)}), f32[48,7]{1,0:T(8,128)}) %reduce-scatter.16.cloned.1.call-update) | async-done | bytes 1360
  612.6 2.5 fusion.71
  615.1 3.3 add_convert_fusion.1
  618.4 394.0 %all-reduce.3.cloned.1.call-done = f32[1,2,3,768,768]{4,1,2,0,3:T(2,128)} async-done(((f32[1,2,3,768,768]{4,1,2,0,3:T(2,128)}), f32[1,2,3,768,768]{4,1,2,0,3:T(2,128)}) %all-reduce.3.cloned.1.call-update) | async-done | bytes 14155792
  1014.8 140.0 %reduce-scatter.14.cloned.1.call-done = f32[1,2,48,768]{3,2,1,0:T(8,128)} async-done(((f32[1,2,768,768]{3,2,1,0:T(8,128)}), f32[1,2,48,768]{3,2,1,0:T(8,128)}) %reduce-scatter.14.cloned.1.call-update) | async-done | bytes 294928 | tf_op jit(solution)/shard_map/reduce_scatter | solution.py:254
  1154.8 141.3 %reduce-scatter.8.cloned.1.call-done = f32[1,2,48,768]{3,2,1,0:T(8,128)} async-done(((f32[1,2,768,768]{3,2,1,0:T(8,128)}), f32[1,2,48,768]{3,2,1,0:T(8,128)}) %reduce-scatter.8.cloned.1.call-update) | async-done | bytes 294928 | tf_op jit(solution)/shard_map/reduce_scatter | solution.py:251
  1296.1 177.2 %reduce-scatter.10.cloned.1.call-done = f32[1,48,3072]{2,1,0:T(8,128)} async-done(((f32[1,768,3072]{2,1,0:T(8,128)}), f32[1,48,3072]{2,1,0:T(8,128)}) %reduce-scatter.10.cloned.1.call-update) | async-done | bytes 589840 | tf_op jit(solution)/shard_map/reduce_scatter | solution.py:252
  1473.3 176.3 %reduce-scatter.12.cloned.1.call-done = f32[1,192,768]{2,1,0:T(8,128)} async-done(((f32[1,3072,768]{2,1,0:T(8,128)}), f32[1,192,768]{2,1,0:T(8,128)}) %reduce-scatter.12.cloned.1.call-update) | async-done | bytes 589840 | tf_op jit(solution)/shard_map/reduce_scatter | solution.py:253
  (242 shorter events, 61.3 us)
Async XLA Ops:
  7.2 2.2 copy-start.43
  7.2 3.0 copy-start.41
  7.2 3.8 copy-start.42
  7.2 108.2 %all-gather.6.cloned.1.call-start = ((), (), s32[]{:S(2)}) async-start(), calls=%async_computation.5 | async-start | bytes 7520256 | tf_op jit(solution)/shard_map/all_gather | solution.py:140
  9.3 2.5 copy-start.44
  9.4 182.9 %all-gather.8.cloned.1.call-start = ((), (), s32[]{:S(2)}) async-start(), calls=%async_computation.6 | async-start | bytes 2506752 | tf_op jit(solution)/shard_map/all_gather | solution.py:141
  10.1 2.5 copy-start.52
  10.1 105.3 %copy-start.19 = (bf16[1,4,128,768]{3,2,1,0:T(8,128)(2,1)S(1)}, bf16[1,4,128,768]{3,2,1,0:T(8,128)(2,1)}, u32[]{:S(2)}) copy-start(bf16[1,4,128,768]{3,2,1,0:T(8,128)(2,1)} %param.10) | copy-start | bytes 2359300
  10.1 252.8 %all-gather.10.cloned.1.call-start = ((), (), s32[]{:S(2)}) async-start(), calls=%async_computation.7 | async-start | bytes 5013504 | tf_op jit(solution)/shard_map/all_gather | solution.py:142
  10.9 334.4 %all-gather.12.cloned.1.call-start = ((), (), s32[]{:S(2)}) async-start(), calls=%async_computation.8 | async-start | bytes 5013504 | tf_op jit(solution)/shard_map/all_gather | solution.py:143
  11.8 397.1 %all-gather.14.cloned.1.call-start = ((), (), s32[]{:S(2)}) async-start(), calls=%async_computation.9 | async-start | bytes 2506752 | tf_op jit(solution)/shard_map/all_gather | solution.py:144
  12.5 598.5 %reduce-scatter.16.cloned.1.call-start = ((), (), s32[]{:S(2)}) async-start(), calls=%async_computation.14 | async-start | bytes 417792
  118.3 3.5 copy-start.46
  118.3 3.5 copy-start.45
  121.3 62.5 %collective-permute-start = (bf16[512,768]{1,0:T(8,128)(2,1)}, bf16[512,768]{1,0:T(8,128)(2,1)S(1)}, u32[]{:S(2)}, u32[]{:S(2)}) collective-permute-start(bf16[512,768]{1,0:T(8,128)(2,1)} %convolution_convert_fusion.7), channel_id=1, source_target_pairs={{0,16},{16,0},{1,17},{17,1},{2,18},{18,2},{3,19},{19,3},{4,20},{20... | collective-permute-start | bytes 2359304 | tf_op jit(solution)/shard_map/ppermute | solution.py:15
  121.3 63.9 %collective-permute-start.1 = (bf16[512,768]{1,0:T(8,128)(2,1)}, bf16[512,768]{1,0:T(8,128)(2,1)S(1)}, u32[]{:S(2)}, u32[]{:S(2)}) collective-permute-start(bf16[512,768]{1,0:T(8,128)(2,1)} %convolution_convert_fusion.5), channel_id=1, source_target_pairs={{0,16},{16,0},{1,17},{17,1},{2,18},{18,2},{3,19},{19,3},{4,20},{20... | collective-permute-start | bytes 2359304 | tf_op jit(solution)/shard_map/ppermute | solution.py:15
  196.0 6.2 copy-start.12
  222.0 1.7 copy-start
  222.0 1.7 copy-start.38
  223.7 1.7 copy-start.47
  224.4 1.6 copy-start.3
  225.1 2.0 copy-start.26
  351.8 1.5 copy-start.7
  353.3 58.0 %collective-permute-start.2 = (bf16[512,768]{1,0:T(8,128)(2,1)}, bf16[512,768]{1,0:T(8,128)(2,1)}, u32[]{:S(2)}, u32[]{:S(2)}) collective-permute-start(bf16[512,768]{1,0:T(8,128)(2,1)} %add_convert_fusion.2), channel_id=1, source_target_pairs={{0,16},{16,0},{1,17},{17,1},{2,18},{18,2},{3,19},{19,3},{4,20},{20... | collective-permute-start | bytes 2359304 | tf_op jit(solution)/shard_map/ppermute | solution.py:15
  408.9 2.5 copy-start.50
  408.9 2.5 copy-start.51
  415.5 3.2 copy-start.54
  415.5 3.2 copy-start.8
  415.5 5.3 slice-start.4
  416.3 2.4 collective-permute-start.3
  416.4 4.3 slice-start.5
  420.2 9.8 slice-start.2
  420.7 9.3 copy-start.21
  420.8 9.3 copy-start.24
  420.8 9.3 slice-start.3
  435.1 2.2 copy-start.48
  444.0 3.5 copy-start.1
  444.0 3.5 copy-start.17
  444.0 3.5 copy-start.39
  447.5 4.8 slice-start
  448.5 1.5 copy-start.31
  448.5 3.8 slice-start.1
  457.8 2.2 copy-start.4
  457.8 2.2 copy-start.10
  461.7 2.2 copy-start.49
  470.5 3.3 copy-start.18
  470.5 3.3 copy-start.37
  478.7 1.8 copy-start.14
  478.7 1.8 copy-start.35
  480.3 2.4 copy-start.27
  480.3 17.6 %collective-permute-start.4 = (bf16[512,768]{0,1:T(8,128)(2,1)}, bf16[512,768]{0,1:T(8,128)(2,1)}, u32[]{:S(2)}, u32[]{:S(2)}) collective-permute-start(bf16[512,768]{0,1:T(8,128)(2,1)} %bitcast.269), channel_id=1, source_target_pairs={{0,16},{16,0},{1,17},{17,1},{2,18},{18,2},{3,19},{19,3},{4,20},{20... | collective-permute-start | bytes 2359304 | tf_op jit(solution)/shard_map/ppermute | solution.py:15
  484.4 15.4 collective-permute-start.5
  487.7 3.1 copy-start.20
  487.7 5.2 copy-start.16
  490.5 521.9 %all-reduce.3.cloned.1.call-start = ((), (), s32[]{:S(2)}) async-start(), calls=%async_computation.15 | async-start | bytes 28311552
  490.8 2.1 copy-start.15
  538.9 615.9 %reduce-scatter.14.cloned.1.call-start = ((), (), s32[]{:S(2)}) async-start(), calls=%async_computation.13 | async-start | bytes 5013504 | tf_op jit(solution)/shard_map/reduce_scatter | solution.py:254
  546.3 3.4 copy-start.6
  546.4 749.7 %reduce-scatter.8.cloned.1.call-start = ((), (), s32[]{:S(2)}) async-start(), calls=%async_computation.10 | async-start | bytes 5013504 | tf_op jit(solution)/shard_map/reduce_scatter | solution.py:251
  547.7 2.0 copy-start.32
  553.1 920.2 %reduce-scatter.10.cloned.1.call-start = ((), (), s32[]{:S(2)}) async-start(), calls=%async_computation.11 | async-start | bytes 10027008 | tf_op jit(solution)/shard_map/reduce_scatter | solution.py:252
  561.8 1087.8 %reduce-scatter.12.cloned.1.call-start = ((), (), s32[]{:S(2)}) async-start(), calls=%async_computation.12 | async-start | bytes 10027008 | tf_op jit(solution)/shard_map/reduce_scatter | solution.py:253
  571.3 1.9 copy-start.33
  612.6 2.5 copy-start.40
  (15 other events, 17.3 us)
Sparse Core Ops, SparseCore 0:
  11.3 104.0 all-gather.5
  118.6 61.6 all-gather.7
  183.7 79.2 all-gather.9
  266.2 79.0 all-gather.11
  347.8 60.9 all-gather.13
  490.6 120.4 reduce-scatter.15
  618.6 393.7 all-reduce.2
  1018.9 135.8 reduce-scatter.13
  1160.5 135.4 reduce-scatter.7
  1303.1 170.1 reduce-scatter.9
  1479.5 169.9 reduce-scatter.11
where the time goes:
time: 1670 us; the launch traced here: 1660 us
  waiting for transfers between devices  1320 us (79%)
  matrix products  141 us (8%)
  local copies, waits for them, and re-layouts  98.6 us (6%)
  blocking collectives  41.3 us (2%)
  other arithmetic  37.9 us (2%)
    unnamed x13, waiting for transfers between devices  429 us
    reduce_scatter x1, waiting for transfers between devices, local(): lax.psum_scatter(grad_ffin[None], 'dp', scatter_dimension=1, tiled=True)  177 us
    reduce_scatter x1, waiting for transfers between devices, local(): lax.psum_scatter(grad_ffout[None], 'dp', scatter_dimension=1, tiled=True)  176 us
    reduce_scatter x1, waiting for transfers between devices, local(): lax.psum_scatter(grad_out, 'dp', scatter_dimension=2, tiled=True)  141 us
    reduce_scatter x1, waiting for transfers between devices, local(): lax.psum_scatter(grad_join[None], 'dp', scatter_dimension=2, tiled=True)  140 us
    all_gather x1, waiting for transfers between devices, local(): lax.all_gather(proj_master.astype(jnp.bfloat16), 'dp', axis=3, tiled=True)  103 us
    all_gather x1, waiting for transfers between devices, local(): lax.all_gather(ffn_out_master.astype(jnp.bfloat16), 'dp', axis=1, tiled=T...  61.3 us
    all_gather x1, waiting for transfers between devices, local(): lax.all_gather(join_master.astype(jnp.bfloat16), 'dp', axis=2, tiled=True)  55.6 us
  transfers between devices with their start and end apart: 17, of which 11 were waited for; matrix products, arithmetic and copies ran while one was open for 12% of the time, Pallas kernels for 0%

commit v1 on v0

--- a/solution.py
+++ b/solution.py
@@ -1,14 +1,1307 @@
+import math
 from functools import partial
 
 import jax
 import jax.numpy as jnp
 from jax import lax
+from jax.experimental import pallas as pl
+from jax.experimental.pallas import tpu as pltpu
 from jax.sharding import PartitionSpec as P
 
 HEADS = 12
 
-
 EPSILON = 1e-05
+VMEM_LIMIT = 62 * 2**20
+TRANSFERS = 300
+MESH = pl.DeviceIdType.MESH
+LOW = jnp.bfloat16
+FULL = jnp.float32
+LINE, PLANE = 4, 4
+RANKS = LINE * PLANE
+HALF = LINE // 2
+KV_CROSS, QO_CROSS, QK_SELF, VO_SELF, JOIN = range(5)
+SQUARES = 5
+FFN_OUT_ROWS, FFN_IN_ROWS = 10, 14
+ITEMS = (
+    (KV_CROSS, 0, 1),
+    (KV_CROSS, 1, 1),
+    (QO_CROSS, 0, 2),
+    (QK_SELF, 0, 2),
+    (VO_SELF, 0, 2),
+    (JOIN, 0, 2),
+    (JOIN, 0, 1),
+    (JOIN, 1, 1),
+)
+VECTORS = None
+H2, FFN, STATE, ERR, FFN_BACK = range(5)
+CORNER_RING, SIDE_RING, LINE_RING, HOP_RING, PAIR_RING = 3, 4, 5, 5, 3
+BLOCK = 64
+KEPT = 112
+TILE = 256
+TILES = tuple(pl.ds(at, TILE) for at in range(0, 768, TILE))
+HEAD = 64
+PAIR = 2 * HEAD
+
+
+class Links:
+    def __init__(self, send_sems, recv_sems):
+        self.stream = lax.axis_index("stream")
+        self.me = lax.axis_index("dp")
+        self.z = self.me // PLANE
+        self.q = self.me % PLANE
+        self.qx = self.q + 1 - 2 * (self.q % 2)
+        self.qy = (self.q + 2) % PLANE
+        self.qd = PLANE - 1 - self.q
+        self.xx, self.yy = self.q % 2, self.q // 2
+        self.columns = (self.q, self.qx, self.qy, self.qd)
+        self.z_near = self.z + 1 - 2 * (self.z % 2)
+        self.z_two = (self.z + 2) % LINE
+        self.z_third = LINE - 1 - self.z
+        self.middle = (self.z == 1) | (self.z == 2)
+        self.x = (self.stream, self.z * PLANE + self.qx)
+        self.y = (self.stream, self.z * PLANE + self.qy)
+        self.near, self.two, self.third = (
+            (self.stream, at * PLANE + self.q) for at in (self.z_near, self.z_two, self.z_third)
+        )
+        self.twin = (1 - self.stream, self.me)
+        self.sems = (send_sems, recv_sems)
+        self.used = 0
+
+    def greet(self):
+        for peer in (self.x, self.y, self.near, self.two, self.third, self.twin):
+            pl.semaphore_signal(
+                pltpu.get_barrier_semaphore(), inc=1, device_id=peer, device_id_type=MESH
+            )
+
+    def met(self):
+        pl.semaphore_wait(pltpu.get_barrier_semaphore(), 6)
+
+    def copy(self, source, target, peer, landing=None):
+        number = self.used
+        self.used += 1
+        return pltpu.make_async_remote_copy(
+            src_ref=source,
+            dst_ref=target,
+            send_sem=self.sems[0].at[number],
+            recv_sem=self.sems[1].at[number if landing is None else landing],
+            device_id=peer,
+            device_id_type=MESH,
+        )
+
+    def send(self, source, target, peer):
+        copy = self.copy(source, target, peer)
+        copy.start()
+        return copy
+
+
+class LineGather:
+    def __init__(self, view, links):
+        self.view, self.k = view, links
+
+    def launch(self):
+        k = self.k
+        own = self.view(k.z)
+        self.near = k.send(own, own, k.near)
+        self.two = k.send(own, own, k.two)
+        landing = k.used
+        self.third = k.copy(own, own, k.third)
+        passed = self.view(k.z_two)
+        self.passed = k.copy(passed, passed, k.near, landing)
+        pl.when(k.middle)(self.third.start)
+
+    def relay(self):
+        self.two.wait_recv()
+        pl.when(self.k.middle)(self.passed.start)
+
+    def arrive(self):
+        self.near.wait_recv()
+        self.third.wait_recv()
+
+    def drain(self):
+        self.near.wait_send()
+        self.two.wait_send()
+
+        @pl.when(self.k.middle)
+        def _():
+            self.third.wait_send()
+            self.passed.wait_send()
+
+
+class LineSum:
+    def __init__(self, view, room, links, straight=False):
+        self.view, self.room, self.k, self.straight = view, room, links, straight
+
+    def launch(self):
+        k = self.k
+        self.spots, self.hop = self.room()
+        self.near = k.send(self.view(k.z_near), self.spots(0), k.near)
+        away = self.view(k.z_third)
+        self.third = k.copy(away, self.spots(2), k.third)
+        if self.straight:
+            self.third.start()
+            self.two = k.send(self.view(k.z_two), self.spots(1), k.two)
+            return
+        self.passed = k.copy(away, self.hop, k.near)
+        pl.when(k.middle)(self.third.start)
+        pl.when(jnp.logical_not(k.middle))(self.passed.start)
+
+    def bridge(self):
+        k = self.k
+        if self.straight:
+            return
+        part = self.view(k.z_two)
+
+        @pl.when(k.middle)
+        def _():
+            self.passed.wait_recv()
+            part[...] = total(part, self.hop).astype(part.dtype)
+
+        self.two = k.send(part, self.spots(1), k.two)
+
+    def collect(self, put):
+        k = self.k
+        self.near.wait_recv()
+        self.two.wait_recv()
+        terms = [self.view(k.z), self.spots(0), self.spots(1)]
+        if self.straight:
+            self.third.wait_recv()
+            put(total(*terms, self.spots(2)))
+            return
+
+        @pl.when(k.middle)
+        def _():
+            self.third.wait_recv()
+            put(total(*terms, self.spots(2)))
+
+        pl.when(jnp.logical_not(k.middle))(lambda: put(total(*terms)))
+
+    def drain(self):
+        self.near.wait_send()
+        self.two.wait_send()
+        if self.straight:
+            self.third.wait_send()
+            return
+        pl.when(self.k.middle)(self.third.wait_send)
+        pl.when(jnp.logical_not(self.k.middle))(self.passed.wait_send)
+
+
+class GatherByLine:
+    def __init__(self, view, links):
+        self.view, self.k = view, links
+        self.line = LineGather(lambda z: view(z, links.q), links)
+
+    def L(self):
+        self.line.launch()
+
+    def R(self):
+        self.line.relay()
+
+    def X(self):
+        k = self.k
+        self.line.arrive()
+        column = self.view(slice(None), k.q)
+        self.sides = [k.send(column, column, k.x), k.send(column, column, k.y)]
+
+    def C(self):
+        k = self.k
+        for copy in self.sides:
+            copy.wait_recv()
+        one, two = self.view(slice(0, HALF), k.qx), self.view(slice(HALF, LINE), k.qy)
+        self.corners = [k.send(one, one, k.y), k.send(two, two, k.x)]
+
+    def F(self):
+        for copy in self.corners:
+            copy.wait_recv()
+        for copy in self.sides + self.corners:
+            copy.wait_send()
+        self.line.drain()
+
+
+class GatherByPlane:
+    def __init__(self, view, links):
+        self.view, self.k = view, links
+        self.lines = [
+            LineGather(partial(lambda q, z: view(z, q), q), links) for q in links.columns
+        ]
+
+    def X(self):
+        k = self.k
+        own = self.view(k.z, k.q)
+        self.sides = [k.send(own, own, k.x), k.send(own, own, k.y)]
+
+    def C(self):
+        k = self.k
+        for copy in self.sides:
+            copy.wait_recv()
+        one, two = self.view(k.z, k.qx, 0, 1), self.view(k.z, k.qy, 1, 1)
+        self.corners = [k.send(one, one, k.y), k.send(two, two, k.x)]
+
+    def L(self, column):
+        if column == 3:
+            for copy in self.corners:
+                copy.wait_recv()
+        self.lines[column].launch()
+
+    def R(self, column):
+        self.lines[column].relay()
+
+    def F(self):
+        for line in self.lines:
+            line.arrive()
+        for line in self.lines:
+            line.drain()
+        for copy in self.sides + self.corners:
+            copy.wait_send()
+
+
+class ScatterByPlane:
+    def __init__(self, view, room, put, links, straight):
+        self.view, self.room, self.put, self.k = view, room, put, links
+        self.line = LineSum(lambda z: view(z, links.q), room.line, links, straight)
+
+    def C(self):
+        k = self.k
+        self.corners, self.sides = self.room.plane()
+        low, high = slice(0, HALF), slice(HALF, LINE)
+        self.one = [
+            k.send(self.view(low, k.qd), self.corners(0), k.x),
+            k.send(self.view(high, k.qd), self.corners(1), k.y),
+        ]
+        self.two = [
+            k.send(self.view(low, k.qx), self.sides(0, low), k.x),
+            k.send(self.view(high, k.qy), self.sides(1, high), k.y),
+        ]
+
+    def X(self):
+        k = self.k
+        low, high = slice(0, HALF), slice(HALF, LINE)
+        for number, half, q in ((0, low, k.qy), (1, high, k.qx)):
+            self.one[number].wait_recv()
+            part = self.view(half, q)
+            part[...] = total(part, self.corners(number)).astype(part.dtype)
+        self.two += [
+            k.send(self.view(high, k.qx), self.sides(0, high), k.x),
+            k.send(self.view(low, k.qy), self.sides(1, low), k.y),
+        ]
+
+    def L(self):
+        k = self.k
+        for copy in self.two:
+            copy.wait_recv()
+        part = self.view(slice(None), k.q)
+        everything = slice(None)
+        part[...] = total(part, self.sides(0, everything), self.sides(1, everything)).astype(part.dtype)
+        self.line.launch()
+
+    def B(self):
+        self.line.bridge()
+
+    def F(self):
+        self.line.collect(self.put.sums)
+        self.put.store()
+        for copy in self.one + self.two:
+            copy.wait_send()
+        self.line.drain()
+
+
+class PairGatherByLine:
+    def __init__(self, view, links, first=None):
+        self.view, self.k, self.first = view, links, first
+        self.line = LineGather(lambda z: view(z, links.yy), links)
+
+    def L(self):
+        if self.first is not None:
+            self.first().wait_recv()
+        self.line.launch()
+
+    def R(self):
+        self.line.relay()
+
+    def X(self):
+        k = self.k
+        self.line.arrive()
+        column = self.view(slice(None), k.yy)
+        self.side = k.send(column, column, k.y)
+
+    def F(self):
+        self.side.wait_recv()
+        self.side.wait_send()
+        self.line.drain()
+        if self.first is not None:
+            self.first().wait_send()
+
+
+class PairGatherByPlane:
+    def __init__(self, view, links):
+        self.view, self.k = view, links
+        self.lines = [
+            LineGather(partial(lambda y, z: view(z, y), y), links) for y in (links.yy, 1 - links.yy)
+        ]
+
+    def X(self):
+        k = self.k
+        own = self.view(k.z, k.yy)
+        self.side = k.send(own, own, k.y)
+
+    def L(self, row):
+        if row == 1:
+            self.side.wait_recv()
+        self.lines[row].launch()
+
+    def R(self, row):
+        self.lines[row].relay()
+
+    def F(self):
+        for line in self.lines:
+            line.arrive()
+        for line in self.lines:
+            line.drain()
+        self.side.wait_send()
+
+
+class PairScatterByPlane:
+    def __init__(self, view, room, put, links):
+        self.view, self.room, self.put, self.k = view, room, put, links
+        self.line = LineSum(lambda z: view(z, links.yy), room.line, links)
+
+    def C(self):
+        k = self.k
+        self.side = self.room.column()
+        self.two = k.send(self.view(slice(None), 1 - k.yy), self.side, k.y)
+
+    def L(self):
+        k = self.k
+        self.two.wait_recv()
+        part = self.view(slice(None), k.yy)
+        part[...] = total(part, self.side).astype(part.dtype)
+        self.line.launch()
+
+    def B(self):
+        self.line.bridge()
+
+    def F(self):
+        self.line.collect(self.put.sums)
+        self.put.store()
+        self.two.wait_send()
+        self.line.drain()
+
+    def G(self):
+        self.put.G()
+
+
+class PairScatterByLine:
+    def __init__(self, view, side, room, put, links):
+        self.view, self.side, self.put, self.k = view, side, put, links
+        self.rows = (1 - links.yy, links.yy)
+        self.lines = [
+            LineSum(partial(lambda y, z: view(z, y), y), room.line, links) for y in self.rows
+        ]
+
+    def L(self, row):
+        self.lines[row].launch()
+
+    def B(self, row):
+        self.lines[row].bridge()
+
+    def M(self, row):
+        part = self.view(self.k.z, self.rows[row])
+
+        def put(value):
+            part[...] = value.astype(part.dtype)
+
+        self.lines[row].collect(put)
+
+    def X(self):
+        k = self.k
+        self.two = k.send(self.view(k.z, 1 - k.yy), self.side, k.y)
+
+    def F(self):
+        k = self.k
+        self.two.wait_recv()
+        self.put.sums(total(self.view(k.z, k.yy), self.side))
+        self.put.store()
+        self.two.wait_send()
+        for line in self.lines:
+            line.drain()
+
+
+def total(*refs):
+    result = refs[0][...].astype(FULL)
+    for ref in refs[1:]:
+        result = result + ref[...].astype(FULL)
+    return result
+
+
+class Room:
+    def __init__(self, size, corners, sides, lines, hops, used):
+        self.size, self.used = size, used
+        self.corners, self.sides, self.lines, self.hops = corners, sides, lines, hops
+
+    def slot(self, ring):
+        number = self.used.setdefault(id(ring), 0)
+        self.used[id(ring)] += 1
+        return ring.at[number % ring.shape[0]]
+
+    def column(self):
+        return self.slot(self.sides)
+
+    def plane(self):
+        corners, sides = self.slot(self.corners), self.slot(self.sides)
+        some = pl.ds(0, self.size)
+        return (lambda n: corners.at[n, :, some]), (lambda n, half: sides.at[half, n, some])
+
+    def line(self):
+        lines, hops = self.slot(self.lines), self.slot(self.hops)
+        some = pl.ds(0, self.size)
+        return (lambda n: lines.at[n, some]), hops.at[some]
+
+
+class VectorRoom(Room):
+    def plane(self):
+        return (lambda n: self.corners.at[n]), (lambda n, half: self.sides.at[n, half])
+
+    def line(self):
+        return (lambda n: self.lines.at[n]), self.hops
+
+
+class Put:
+    def __init__(self, stage, targets, sems, first):
+        self.stage, self.targets, self.sems, self.first = stage, targets, sems, first
+        self.copies = []
+
+    def sums(self, values):
+        for i in range(len(self.targets)):
+            self.stage(i)[...] = values[i]
+
+    def store(self):
+        for i, target in enumerate(self.targets):
+            copy = pltpu.make_async_copy(self.stage(i), target, self.sems.at[self.first + i])
+            copy.start()
+            self.copies.append(copy)
+
+
+class PutVectors:
+    def __init__(self, target):
+        self.target, self.copies = target, []
+
+    def sums(self, values):
+        rows, _, width = self.target.shape
+        for row in range(rows):
+            self.target[row] = values[row : row + 1, :width]
+
+    def store(self):
+        pass
+
+
+def layer_kernel(
+    rows,
+    lengths,
+    drops,
+    x_in,
+    cot_in,
+    proj,
+    outw,
+    fin,
+    fout,
+    join,
+    vec,
+    joined,
+    x_grad,
+    proj_g,
+    out_g,
+    fin_g,
+    fout_g,
+    join_g,
+    vec_g,
+    sq,
+    fi,
+    wd,
+    halves,
+    vecs,
+    corners,
+    sides,
+    lines,
+    hops,
+    side_room,
+    pair_lines,
+    pair_hops,
+    vcorners,
+    vsides,
+    vlines,
+    vhop,
+    vw,
+    vg,
+    part,
+    x,
+    cot,
+    nothing,
+    h2a,
+    ea,
+    act,
+    mid,
+    slope,
+    probs,
+    unit,
+    inv,
+    work,
+    load_sems,
+    page_sems,
+    store_sems,
+    send_sems,
+    recv_sems,
+    ready,
+):
+    k = Links(send_sems, recv_sems)
+    width = sq.shape[-1]
+    count = x.shape[0]
+    pages, slots = x_in.shape[:2]
+    pairs = width // PAIR
+    scale = HEAD**-0.5
+    (k1, v1, q1, o1, h1, q2, k2, v2, o2, state, far, edge, back) = range(13)
+    mine, theirs = pl.ds(0, count), pl.ds(count, count)
+    acc, res, grd = (work.at[pl.ds(i * count, count)] for i in range(3))
+
+    def weight(group, index):
+        return sq[group, :, :, index].reshape(width, width)
+
+    def in_weight(block):
+        return fi[:, :, block].reshape(width, width)
+
+    def out_weight(block):
+        return wd[2 * block : 2 * block + 2].reshape(width, width)
+
+    def free(slot):
+        return mid.at[slot // 2, pl.ds((slot % 2) * count, count)]
+
+    def spare(slot):
+        return slope.at[slot // 2, pl.ds((slot % 2) * count, count)]
+
+    def times(left, right):
+        return jnp.dot(left, right, preferred_element_type=FULL)
+
+    def times_transposed(left, right):
+        return lax.dot_general(left, right, (((1,), (1,)), ((), ())), preferred_element_type=FULL)
+
+    def outer(left, right):
+        return lax.dot_general(left, right, (((0,), (0,)), ((), ())), preferred_element_type=FULL)
+
+    def loop(first, last, body):
+        def step(i, carry):
+            body(i)
+            return carry
+
+        lax.fori_loop(first, last, step, 0)
+
+    def by_rows(body, first=0, last=None):
+        def step(i):
+            body(pl.ds(pl.multiple_of(i * BLOCK, BLOCK), BLOCK), i)
+
+        loop(first, count // BLOCK if last is None else last, step)
+
+    def rows_of(i):
+        return lax.broadcasted_iota(jnp.int32, (BLOCK, 1), 0) + i * BLOCK
+
+    def narrow(source, target):
+        def step(at, i):
+            del i
+            target[at] = source[at].astype(LOW)
+
+        by_rows(step)
+
+    def row_mask(i):
+        row, mask = rows_of(i), jnp.zeros((BLOCK, 1), FULL)
+        for page in range(pages):
+            first = page * KEPT
+            mask = jnp.where((row >= first) & (row < first + lengths[page]), 1.0, mask)
+        return mask
+
+    def keep(i):
+        row, kept = rows_of(i), jnp.zeros((BLOCK, 1), FULL)
+        for page in range(pages):
+            kept = jnp.where(row >= page * KEPT, (1 - drops[page]).astype(FULL), kept)
+        return kept
+
+    def rows_in(slot):
+        return act.at[slot, pl.ds(0, count)]
+
+    def vector(row):
+        return vw[row : row + 1, :]
+
+    def norm(number, at, values):
+        centre = values - jnp.mean(values, axis=-1, keepdims=True)
+        inverse = lax.rsqrt(jnp.mean(centre * centre, axis=-1, keepdims=True) + EPSILON)
+        plain = centre * inverse
+        unit[number, at] = plain.astype(LOW)
+        inv[number, at] = inverse
+        return plain * vector(2 * number) + vector(2 * number + 1)
+
+    def fold(values):
+        return jnp.sum(values.reshape(BLOCK // 8, 8, width), axis=0)
+
+    def norm_back(number, grad, after):
+        part[...] = jnp.zeros_like(part)
+
+        def step(at, i):
+            value = grad(at)
+            plain = unit[number, at].astype(FULL)
+            part[0] += fold(value * plain)
+            part[1] += fold(value)
+            scaled = value * vector(2 * number)
+            inner = (
+                scaled
+                - jnp.mean(scaled, axis=-1, keepdims=True)
+                - plain * jnp.mean(scaled * plain, axis=-1, keepdims=True)
+            )
+            result = inv[number, at] * inner
+            grd[at] = result
+            after(at, i, result)
+
+        by_rows(step)
+        for i in range(2):
+            vg[2 * number + i : 2 * number + i + 1, :] = jnp.sum(part[i], axis=0, keepdims=True)
+
+    def split_heads(values):
+        first = lax.broadcasted_iota(jnp.int32, values.shape, 1) < HEAD
+        zero = jnp.zeros_like(values)
+        return jnp.concatenate([jnp.where(first, values, zero), jnp.where(first, zero, values)], axis=0)
+
+    def join_heads(values):
+        first = lax.broadcasted_iota(jnp.int32, (KEPT, PAIR), 1) < HEAD
+        return jnp.where(first, values[:KEPT], values[KEPT:])
+
+    def by_heads(half, body):
+        group = 3
+
+        def step(i):
+            page = i // (pairs // group)
+            start = pl.multiple_of(page * KEPT, KEPT)
+            at, keys_at = pl.ds(start, KEPT), pl.ds(start, slots)
+            for j in range(group):
+                pair = (i % (pairs // group)) * group + j
+                lanes = pl.ds(pl.multiple_of(pair * PAIR, PAIR), PAIR)
+                body(page, at, keys_at, lanes, i * group + j)
+
+        steps = pages * (pairs // group)
+        loop(half * (steps // 2), steps if half else steps // 2, step)
+
+    def attend(half, which, query, keys, values, result):
+        def body(page, at, keys_at, lanes, number):
+            scores = times_transposed(split_heads(act[query, at, lanes]), act[keys, keys_at, lanes]) * scale
+            spot = lax.broadcasted_iota(jnp.int32, scores.shape, 1)
+            scores = jnp.where(spot < lengths[page], scores, -1e30)
+            weights = jnp.exp(scores - jnp.max(scores, axis=-1, keepdims=True))
+            chance = weights * (1.0 / jnp.sum(weights, axis=-1, keepdims=True))
+            chance = chance.astype(LOW)
+            probs[which, number] = chance
+            act[result, at, lanes] = join_heads(times(chance, act[values, keys_at, lanes])).astype(LOW)
+
+        by_heads(half, body)
+
+    def attend_back(half, which, query, keys, values):
+        grad, to_query, to_keys, to_values = free(0), spare(0), spare(1), spare(2)
+
+        def body(page, at, keys_at, lanes, number):
+            del page
+            chance = probs[which, number]
+            spread = split_heads(grad[at, lanes])
+            pull = times_transposed(spread, act[values, keys_at, lanes])
+            wide_chance = chance.astype(FULL)
+            inner = pull - jnp.sum(pull * wide_chance, axis=-1, keepdims=True)
+            delta = (wide_chance * inner).astype(LOW)
+            to_query[at, lanes] = (join_heads(times(delta, act[keys, keys_at, lanes])) * scale).astype(LOW)
+            key_grad = outer(delta, split_heads(act[query, at, lanes]))[:KEPT]
+            to_keys[at, lanes] = (key_grad * scale).astype(LOW)
+            to_values[at, lanes] = outer(chance, spread)[:KEPT].astype(LOW)
+
+        by_heads(half, body)
+
+    def square_grad(group, index, left, right):
+        sq[group, :, :, index] = outer(left, right).astype(LOW).reshape(LINE, PLANE, rows, width)
+
+    def view(item):
+        if item is VECTORS:
+            return lambda z, q: vecs.at[z, q]
+        group, start, size = item
+        return lambda z, q, first=0, some=size: sq.at[group, z, q, pl.ds(start + first, some)]
+
+    def outputs(item):
+        group, start, size = item
+        places = []
+        for i in range(start, start + size):
+            if group == JOIN:
+                places.append(join_g.at[i])
+            elif group == KV_CROSS:
+                places.append(proj_g.at[1 + i])
+            elif group == QK_SELF:
+                places.append(proj_g.at[3 + i])
+            elif i == 1:
+                places.append(out_g.at[0 if group == QO_CROSS else 1])
+            else:
+                places.append(proj_g.at[0 if group == QO_CROSS else 5])
+        return places
+
+    def put_for(item):
+        if item is VECTORS:
+            return PutVectors(vec_g)
+        first = 2 * item[0] + item[1]
+        return Put(lambda i: work.at[pl.ds((first + i) * rows, rows)], outputs(item), store_sems, first)
+
+    used = {}
+
+    def gather(item, by=GatherByLine):
+        return by(view(item), k)
+
+    def keep_scatter(item):
+        scatters.append(item)
+        return item
+
+    def scatter(item, straight=False):
+        if item is VECTORS:
+            room = VectorRoom(0, vcorners, vsides, vlines, vhop, used)
+        else:
+            room = Room(item[2], corners, sides, lines, hops, used)
+        return keep_scatter(ScatterByPlane(view(item), room, put_for(item), k, straight))
+
+    def out_view(z, y):
+        return wd.at[z, y]
+
+    def in_view(z, y):
+        return fi.at[z, pl.ds(2 * y, 2)]
+
+    def stage_of(first):
+        return lambda i: work.at[pl.ds((first + i) * rows, rows)]
+
+    class PutOut(Put):
+        def sums(self, values):
+            for i in range(4):
+                self.stage(i)[...] = values[i // 2, i % 2]
+
+    class PutIn(Put):
+        def sums(self, values):
+            for i in range(4):
+                self.stage(i)[...] = values[i // 2, i % 2]
+
+        def two_rows(self, first, x_):
+            return work.at[pl.ds(pl.multiple_of((first + 2 * x_) * rows, rows), 2 * rows)]
+
+        def half(self, h, block):
+            return work[(2 * h + block) * rows : (2 * h + block + 1) * rows]
+
+        def store(self):
+            self.two_rows(0, k.xx)[...] = self.two_rows(FFN_IN_ROWS, k.xx)[...]
+            other = self.two_rows(FFN_IN_ROWS, 1 - k.xx)[...]
+            halves[0] = other.astype(LOW).reshape(2, rows, width)
+            self.swap = k.send(halves.at[0], halves.at[1], k.x)
+
+        def G(self):
+            self.swap.wait()
+            other = halves[1].astype(FULL).reshape(2 * rows, width)
+            self.two_rows(0, 1 - k.xx)[...] = other
+            piece = width // 4
+            for j in range(4):
+                block, first = j // 2, (j % 2) * 2 * piece
+                parts = [
+                    self.half(h, block)[:, first + g * piece : first + (g + 1) * piece]
+                    for g in range(2)
+                    for h in range(2)
+                ]
+                self.stage(j)[...] = jnp.concatenate(parts, axis=1)
+            Put.store(self)
+
+    scatters = []
+    pair_room = Room(2, corners, sides, pair_lines, pair_hops, used)
+    put_out = PutOut(
+        stage_of(FFN_OUT_ROWS),
+        [fout_g.at[pl.ds(i * rows, rows)] for i in range(4)],
+        store_sems,
+        FFN_OUT_ROWS,
+    )
+    put_in = PutIn(
+        stage_of(FFN_IN_ROWS),
+        [fin_g.at[:, pl.ds(i * width, width)] for i in range(4)],
+        store_sems,
+        FFN_IN_ROWS,
+    )
+    gFO = PairGatherByPlane(out_view, k)
+    gFI = PairGatherByLine(in_view, k, lambda: swaps["in"])
+    sFO = keep_scatter(PairScatterByLine(out_view, side_room, pair_room, put_out, k))
+    sFI = keep_scatter(PairScatterByPlane(in_view, pair_room, put_in, k))
+    gK = gather(ITEMS[0])
+    gV = gather(ITEMS[1])
+    gQO = gather(ITEMS[2])
+    gQK = gather(ITEMS[3])
+    gVO = gather(ITEMS[4])
+    gJ = gather(ITEMS[5], GatherByPlane)
+    gvec = gather(VECTORS)
+    sK = scatter(ITEMS[0])
+    sV = scatter(ITEMS[1])
+    sQO = scatter(ITEMS[2])
+    sQK = scatter(ITEMS[3])
+    sVO = scatter(ITEMS[4])
+    sJ0 = scatter(ITEMS[6])
+    sJ1 = scatter(ITEMS[7])
+    svec = scatter(VECTORS)
+    swaps = {}
+
+    def swap(name, source, target, peer=None):
+        swaps[name] = k.send(source, target, k.twin if peer is None else peer)
+
+    def swapped(*names):
+        for name in names:
+            swaps[name].wait()
+
+    sources, first = [], 0
+    for shard in (proj, outw, join, fout):
+        sources.append((shard, pl.ds(first, shard.shape[0])))
+        first += shard.shape[0]
+    for j in range(4):
+        sources.append((fin.at[:, pl.ds(j * width, width)], pl.ds(first, rows)))
+        first += rows
+    loads = [
+        pltpu.make_async_copy(source, work.at[at], load_sems.at[i])
+        for i, (source, at) in enumerate(sources)
+    ]
+
+    page_loads = [
+        pltpu.make_async_copy(
+            source.at[page, pl.ds(0, KEPT)],
+            target.at[pl.ds(page * KEPT, KEPT)],
+            page_sems.at[number * pages + page],
+        )
+        for number, (source, target) in enumerate(((x_in, x), (cot_in, cot)))
+        for page in range(pages)
+    ]
+    page_copies = []
+
+    def pages_out(source, target, number):
+        for page in range(pages):
+            for i, (piece, at) in enumerate(
+                (
+                    (source.at[pl.ds(page * KEPT, KEPT)], pl.ds(0, KEPT)),
+                    (nothing, pl.ds(KEPT, slots - KEPT)),
+                )
+            ):
+                sem = page_sems.at[2 * pages + (number * pages + page) * 2 + i]
+                copy = pltpu.make_async_copy(piece, target.at[page, at], sem)
+                copy.start()
+                page_copies.append(copy)
+
+    def cast(number):
+        return work[number * rows : (number + 1) * rows].astype(LOW)
+
+    def place(*blocks):
+        for group, index, number in blocks:
+            sq[group, k.z, k.q, index] = cast(number)
+
+    def place_out():
+        for j in range(4):
+            wd[k.z, k.yy, j // 2, j % 2] = cast(FFN_OUT_ROWS + j)
+
+    def place_in():
+        piece = width // 4
+        for h in range(2):
+            for block in range(2):
+                parts = [
+                    cast(FFN_IN_ROWS + 2 * block + j)[:, (2 * g + h) * piece : (2 * g + h + 1) * piece]
+                    for j in range(2)
+                    for g in range(2)
+                ]
+                halves[h, block] = jnp.concatenate(parts, axis=1)
+        fi[k.z, k.q] = halves[k.xx]
+        swap("in", halves.at[1 - k.xx], fi.at[k.z, k.q], k.x)
+
+    def start():
+        k.greet()
+        for copy in loads + page_loads:
+            copy.start()
+        vecs[k.z, k.q] = jnp.zeros(vecs.shape[2:], FULL)
+        for row in range(vec.shape[0]):
+            vecs[k.z, k.q, row : row + 1, :rows] = vec[row]
+        loads[0].wait()
+        place((KV_CROSS, 0, 1), (KV_CROSS, 1, 2))
+        k.met()
+
+    def cast1():
+        loads[2].wait()
+        loads[3].wait()
+        place((JOIN, 0, 8), (JOIN, 1, 9))
+        place_out()
+
+    def cast2():
+        for copy in (loads[1], *loads[4:], *page_loads):
+            copy.wait()
+        place((QO_CROSS, 0, 0), (QO_CROSS, 1, 6), (QK_SELF, 0, 3), (QK_SELF, 1, 4))
+        place((VO_SELF, 0, 5), (VO_SELF, 1, 7))
+        place_in()
+        nothing[...] = jnp.zeros_like(nothing)
+        for one in (k1, v1, k2, v2):
+            act[one, pl.ds(count, slots - KEPT)] = jnp.zeros((slots - KEPT, width), LOW)
+
+    def kv0():
+        free(0)[...] = times(x[...], weight(KV_CROSS, 0)).astype(LOW)
+        swap("keys", free(0), rows_in(k1))
+
+    def kv1():
+        free(1)[...] = times(x[...], weight(KV_CROSS, 1)).astype(LOW)
+        swap("values", free(1), rows_in(v1))
+
+    def vectors():
+        sums = jnp.zeros((8, width), FULL)
+        zeros = jnp.zeros((8, width - 128), FULL)
+        for d in range(RANKS):
+            tile = jnp.concatenate([vecs[d // PLANE, d % PLANE], zeros], axis=1)
+            sums = sums + (pltpu.roll(tile, d * rows, 1) if d else tile)
+        vw[...] = sums.astype(LOW).astype(FULL)
+
+    def project_q1():
+        rows_in(q1)[...] = times(x[...], weight(QO_CROSS, 0)).astype(LOW)
+        swapped("keys", "values")
+
+    def ln1():
+        acc[...] = times(rows_in(o1)[...], weight(QO_CROSS, 1))
+
+        def step(at, i):
+            value = norm(0, at, x[at].astype(FULL) + acc[at] * keep(i))
+            res[at] = value
+            act[h1, at] = value.astype(LOW)
+
+        by_rows(step)
+
+    def project_self(slot_, group, index):
+        rows_in(slot_)[...] = times(rows_in(h1)[...], weight(group, index)).astype(LOW)
+
+    def in_two(step, name, buffer, target, peer):
+        half = (count // BLOCK + 1) // 2
+        for number, first, last in ((0, 0, half), (1, half, count // BLOCK)):
+            by_rows(step, first, last)
+            at = pl.ds(first * BLOCK, (last - first) * BLOCK)
+            swap((name, number), buffer.at[at], target.at[at], peer)
+
+    def ln2():
+        acc[...] = times(rows_in(o2)[...], weight(VO_SELF, 1))
+
+        def step(at, i):
+            del i
+            value = norm(1, at, res[at] + acc[at])
+            res[at] = value
+            h2a[at] = value.astype(LOW)
+
+        in_two(step, H2, h2a, h2a.at[theirs], k.x)
+
+    def ffn_in(whose, block):
+        if whose is theirs and block == 0:
+            swapped((H2, 0), (H2, 1))
+        first = 0 if whose is mine else count
+        acc[...] = times(h2a[whose], in_weight(block))
+
+        def step(at, i):
+            value = acc[at]
+            share = 0.5 + 0.5 * lax.erf(value * (0.5**0.5))
+            bell = jnp.exp(value * value * -0.5) * (1.0 / (2.0 * math.pi) ** 0.5)
+            to = pl.ds(pl.multiple_of(first + i * BLOCK, BLOCK), BLOCK)
+            mid[block, to] = (value * share).astype(LOW)
+            slope[block, to] = (share + value * bell).astype(LOW)
+
+        by_rows(step)
+
+    def ffn_out_theirs():
+        acc[...] = times(mid[0, theirs], out_weight(0))
+        acc[...] += times(mid[1, theirs], out_weight(1))
+        narrow(acc, rows_in(edge))
+        swap(FFN, rows_in(edge), rows_in(back), k.x)
+
+    def ffn_out_mine():
+        for block in range(2):
+            res[...] += times(mid[block, mine], out_weight(block))
+
+    def ln3():
+        swapped(FFN)
+
+        def step(at, i):
+            del i
+            value = res[at] + act[back, at].astype(FULL)
+            act[state, at] = norm(2, at, value).astype(LOW)
+
+        in_two(step, STATE, rows_in(state), rows_in(far), k.twin)
+
+    def join_own():
+        acc[...] = times(rows_in(state)[...], weight(JOIN, 0))
+
+    def join_far():
+        swapped((STATE, 0), (STATE, 1))
+        acc[...] += times(rows_in(far)[...], weight(JOIN, 1))
+
+    def gate():
+        part[...] = jnp.zeros_like(part)
+
+        def step(at, i):
+            own = act[state, at].astype(FULL)
+            other = act[far, at].astype(FULL)
+            share = jax.nn.sigmoid(acc[at] + vector(6))
+            mask = row_mask(i)
+            grad = cot[at].astype(FULL) * mask
+            cot[at] = ((share * own + (1.0 - share) * other) * mask).astype(LOW)
+            to_own, to_other = grad * share, grad * (1.0 - share)
+            logits = (to_own * (own - other) * (1.0 - share)).astype(LOW)
+            ea[at] = logits
+            part[0] += fold(logits.astype(FULL))
+            res[at] = to_own
+            grd[at] = to_other
+
+        by_rows(step)
+        vg[6:7, :] = jnp.sum(part[0], axis=0, keepdims=True)
+        vg[7:8, :] = jnp.zeros((1, width), FULL)
+        pages_out(cot, joined, 0)
+
+    def join_back():
+        logits = ea.at[mine]
+        rows_in(edge)[...] = (grd[...] + times_transposed(logits[...], weight(JOIN, 1))).astype(LOW)
+        swap("edge", rows_in(edge), rows_in(back))
+        square_grad(JOIN, 1, rows_in(far)[...], logits[...])
+
+    def join_back_own():
+        logits = ea.at[mine]
+        res[...] += times_transposed(logits[...], weight(JOIN, 0))
+        square_grad(JOIN, 0, rows_in(state)[...], logits[...])
+
+    def keep_err(at, i, result):
+        del i
+        ea[at] = result.astype(LOW)
+
+    def keep_branch(at, i, result):
+        ea[at] = (result * keep(i)).astype(LOW)
+
+    def ln3_back():
+        swapped("edge")
+        norm_back(2, lambda at: res[at] + act[back, at].astype(FULL), keep_err)
+        swap(ERR, ea.at[mine], ea.at[theirs], k.x)
+
+    def hidden_back(whose, block):
+        if whose is theirs and block == 0:
+            swapped(ERR)
+        first = 0 if whose is mine else count
+        acc[...] = times_transposed(ea[whose], out_weight(block))
+
+        def step(at, i):
+            to = pl.ds(pl.multiple_of(first + i * BLOCK, BLOCK), BLOCK)
+            slope[block, to] = (acc[at] * slope[block, to].astype(FULL)).astype(LOW)
+
+        by_rows(step)
+
+    def out_grad(block):
+        for at in TILES:
+            grad = outer(mid[block], ea[:, at]).astype(LOW)
+            wd[2 * block : 2 * block + 2, :, :, :, :, at] = grad.reshape(2, 2, 2, 2, rows, TILE)
+        if block == 1:
+            pl.semaphore_signal(ready, inc=1, device_id=k.twin, device_id_type=MESH)
+
+    def ffn_in_back_theirs():
+        acc[...] = times_transposed(slope[0, theirs], in_weight(0))
+        acc[...] += times_transposed(slope[1, theirs], in_weight(1))
+        narrow(acc, rows_in(edge))
+        swap(FFN_BACK, rows_in(edge), rows_in(far), k.x)
+
+    def ffn_in_back_mine():
+        for block in range(2):
+            grd[...] += times_transposed(slope[block, mine], in_weight(block))
+
+    def in_grad(block):
+        for at in TILES:
+            grad = outer(h2a[...], slope[block, :, at]).astype(LOW)
+            fi[:, :, block, :, at] = grad.reshape(LINE, PLANE, rows, TILE)
+
+    def ln2_back():
+        swapped(FFN_BACK)
+        norm_back(1, lambda at: grd[at] + act[far, at].astype(FULL), keep_err)
+        free(0)[...] = times_transposed(ea[mine], weight(VO_SELF, 1)).astype(LOW)
+        square_grad(VO_SELF, 1, rows_in(o2)[...], ea[mine])
+
+    def self_back(group, index, which):
+        grd[...] += times_transposed(spare(which)[...], weight(group, index))
+        square_grad(group, index, rows_in(h1)[...], spare(which)[...])
+
+    def ln1_back():
+        norm_back(0, lambda at: grd[at], keep_branch)
+        for d in range(RANKS):
+            moved = pltpu.roll(vg[...], width - d * rows, 1) if d else vg[...]
+            vecs[d // PLANE, d % PLANE] = moved[:, :128]
+        free(0)[...] = times_transposed(ea[mine], weight(QO_CROSS, 1)).astype(LOW)
+        square_grad(QO_CROSS, 1, rows_in(o1)[...], ea[mine])
+
+    def cross_query_back():
+        pl.semaphore_wait(ready, 1)
+        swap("back_keys", spare(1), free(2))
+        swap("back_values", spare(2), free(3))
+        grd[...] += times_transposed(spare(0)[...], weight(QO_CROSS, 0))
+        square_grad(QO_CROSS, 0, x[...], spare(0)[...])
+
+    def cross_back(index):
+        swapped(("back_keys", "back_values")[index])
+        grd[...] += times_transposed(free(2 + index)[...], weight(KV_CROSS, index))
+        square_grad(KV_CROSS, index, x[...], free(2 + index)[...])
+
+    def last_cross_back():
+        cross_back(1)
+        narrow(grd, ea)
+        pages_out(ea.at[mine], x_grad, 1)
+
+    start(); gV.L(); gvec.L(); cast1(); gJ.X(); gK.L(); gFO.X(); cast2(); gV.R(); gvec.R(); gQO.L(); gK.R(); gV.X()
+    gvec.X(); gK.X(); gQK.L(); gJ.C(); gVO.L(); gV.C(); gvec.C(); gK.C(); gQO.R(); gQO.X(); gK.F(); gFI.L(); kv0()
+    gV.F(); gvec.F(); vectors(); gQK.R(); gQK.X(); gQO.C(); gVO.R(); gFI.R(); gFO.L(0); gJ.L(2); kv1(); gVO.X()
+    gQO.F(); gQK.C(); gFO.L(1); gVO.C(); project_q1(); attend(0, 0, q1, k1, v1, o1); gFI.X(); gQK.F()
+    attend(1, 0, q1, k1, v1, o1); gJ.L(3); ln1(); project_self(q2, QK_SELF, 0); gFO.R(0); gVO.F()
+    project_self(k2, QK_SELF, 1); project_self(v2, VO_SELF, 0); attend(0, 1, q2, k2, v2, o2)
+    attend(1, 1, q2, k2, v2, o2); ln2(); gJ.L(1); gFO.R(1); gJ.L(0); gFI.F(); ffn_in(mine, 0); gJ.R(3)
+    ffn_in(mine, 1); ffn_in(theirs, 0); ffn_in(theirs, 1); gFO.F(); gJ.R(2); ffn_out_theirs(); ffn_out_mine()
+    gJ.R(0); gJ.R(1); ln3(); gJ.F(); join_own(); join_far(); gate(); join_back(); sJ1.C(); join_back_own()
+    ln3_back(); hidden_back(mine, 1); hidden_back(mine, 0); ffn_in_back_mine(); sJ1.X(); sJ0.C()
+    hidden_back(theirs, 0); hidden_back(theirs, 1); ffn_in_back_theirs(); sJ1.L(); out_grad(0); in_grad(1); sJ0.X()
+    sJ1.B(); in_grad(0); sFI.C(); out_grad(1); sFO.L(0); ln2_back(); sFO.L(1); attend_back(0, 1, q2, k2, v2)
+    sJ1.F(); attend_back(1, 1, q2, k2, v2); self_back(VO_SELF, 0, 2); sJ0.L(); sVO.C(); sFO.B(0)
+    self_back(QK_SELF, 0, 0); self_back(QK_SELF, 1, 1); sFI.L(); sQK.C(); ln1_back(); sFO.B(1)
+    attend_back(0, 0, q1, k1, v1); sVO.X(); sJ0.B(); sQK.X(); attend_back(1, 0, q1, k1, v1); sFI.B()
+    cross_query_back(); sQO.C(); svec.C(); sJ0.F(); sVO.L(); sQK.L(); cross_back(0); sQO.X(); svec.X(); sQK.B()
+    last_cross_back(); sVO.B(); sK.C(); sQO.L(); svec.L(); sFO.M(0); sV.C(); sQO.B(); svec.B(); sK.X(); sV.X()
+    sQK.F(); sFO.M(1); sFI.F(); sFO.X(); sK.L(); sV.L(); sK.B(); sFI.G(); sV.B(); sQO.F(); svec.F(); sFO.F(); sK.F()
+    sVO.F(); sV.F()
+    for copy in page_copies:
+        copy.wait()
+    for item in scatters:
+        for copy in item.put.copies:
+            copy.wait()
+
+
+def hand_over(count, *refs):
+    sources, targets, rooms, sems = refs[:count], refs[count : 2 * count], refs[2 * count : -1], refs[-1]
+    loads = [
+        pltpu.make_async_copy(source, room, sems.at[0, i])
+        for i, (source, room) in enumerate(zip(sources, rooms))
+    ]
+    stores = [
+        pltpu.make_async_copy(room, target, sems.at[1, i])
+        for i, (room, target) in enumerate(zip(rooms, targets))
+    ]
+    for copy in loads:
+        copy.start()
+    for load, copy in zip(loads, stores):
+        load.wait()
+        copy.start()
+    for copy in stores:
+        copy.wait()
+
+
+def run_layer(x_in, lengths, drops, proj, outw, fin, fout, join, vectors, cot):
+    pages, slots, width = x_in.shape[1:]
+    rows = proj.shape[3]
+    count = pages * KEPT
+    vec = jnp.transpose(vectors, (1, 0, 2))
+    vmem = pl.BlockSpec(memory_space=pltpu.VMEM)
+    smem = pl.BlockSpec(memory_space=pltpu.SMEM)
+    hbm = pl.BlockSpec(memory_space=pl.ANY)
+    slab = (2, rows, width)
+    scratch = [
+        pltpu.VMEM((SQUARES, LINE, PLANE) + slab, LOW),
+        pltpu.VMEM((LINE, PLANE) + slab, LOW),
+        pltpu.VMEM((LINE, 2, 2) + slab, LOW),
+        pltpu.VMEM((2,) + slab, LOW),
+        pltpu.VMEM((LINE, PLANE, 8, 128), FULL),
+        pltpu.VMEM((CORNER_RING, 2, HALF) + slab, LOW),
+        pltpu.VMEM((SIDE_RING, LINE, 2) + slab, LOW),
+        pltpu.VMEM((LINE_RING, LINE - 1) + slab, LOW),
+        pltpu.VMEM((HOP_RING,) + slab, LOW),
+        pltpu.VMEM((2,) + slab, LOW),
+        pltpu.VMEM((PAIR_RING, LINE - 1, 2) + slab, LOW),
+        pltpu.VMEM((PAIR_RING, 2) + slab, LOW),
+        pltpu.VMEM((2, HALF, 8, 128), FULL),
+        pltpu.VMEM((2, LINE, 8, 128), FULL),
+        pltpu.VMEM((LINE - 1, 8, 128), FULL),
+        pltpu.VMEM((8, 128), FULL),
+        pltpu.VMEM((8, width), FULL),
+        pltpu.VMEM((8, width), FULL),
+        pltpu.VMEM((2, 8, width), FULL),
+        pltpu.VMEM((count, width), LOW),
+        pltpu.VMEM((count, width), LOW),
+        pltpu.VMEM((slots - KEPT, width), LOW),
+        pltpu.VMEM((2 * count, width), LOW),
+        pltpu.VMEM((2 * count, width), LOW),
+        pltpu.VMEM((13, count + slots - KEPT, width), LOW),
+        pltpu.VMEM((2, 2 * count, width), LOW),
+        pltpu.VMEM((2, 2 * count, width), LOW),
+        pltpu.VMEM((2, pages * (width // PAIR), 2 * KEPT, slots), LOW),
+        pltpu.VMEM((3, count, width), LOW),
+        pltpu.VMEM((3, count, 1), FULL),
+        pltpu.VMEM((3 * count, width), FULL),
+        pltpu.SemaphoreType.DMA((8,)),
+        pltpu.SemaphoreType.DMA((6 * pages,)),
+        pltpu.SemaphoreType.DMA((18,)),
+        pltpu.SemaphoreType.DMA((TRANSFERS,)),
+        pltpu.SemaphoreType.DMA((TRANSFERS,)),
+        pltpu.SemaphoreType.REGULAR,
+    ]
+    shapes = (
+        ((pages, slots, width), LOW),
+        ((pages, slots, width), LOW),
+        ((6, rows, width), FULL),
+        ((2, rows, width), FULL),
+        ((rows, 4 * width), FULL),
+        ((4 * rows, width), FULL),
+        ((2, rows, width), FULL),
+        ((vectors.shape[1], 1, rows), FULL),
+    )
+    results = pl.pallas_call(
+        partial(layer_kernel, rows),
+        out_shape=[jax.ShapeDtypeStruct(*shape) for shape in shapes],
+        in_specs=[smem, smem] + [hbm] * 7 + [vmem],
+        out_specs=[hbm] * 7 + [vmem],
+        scratch_shapes=scratch,
+        compiler_params=pltpu.CompilerParams(
+            collective_id=0, has_side_effects=True, vmem_limit_bytes=VMEM_LIMIT
+        ),
+    )(
+        lengths,
+        drops,
+        x_in[0],
+        cot[0],
+        proj.reshape(6 * rows, width),
+        outw.reshape(2 * rows, width),
+        fin[0],
+        fout[0],
+        join.reshape(2 * rows, width),
+        vec,
+    )
+    results = pl.pallas_call(
+        partial(hand_over, len(shapes)),
+        out_shape=[jax.ShapeDtypeStruct(*shape) for shape in shapes],
+        in_specs=[hbm] * len(shapes),
+        out_specs=[hbm] * len(shapes),
+        scratch_shapes=[pltpu.VMEM(*shape) for shape in shapes]
+        + [pltpu.SemaphoreType.DMA((2, len(shapes)))],
+        compiler_params=pltpu.CompilerParams(vmem_limit_bytes=VMEM_LIMIT),
+    )(*results)
+    joined, x_grad, proj_g, out_g, fin_g, fout_g, join_g, vec_g = results
+    return (
+        joined[None],
+        x_grad[None],
+        proj_g.reshape(proj.shape),
+        out_g[None],
+        fin_g[None],
+        fout_g[None],
+        join_g[None],
+        jnp.transpose(vec_g, (1, 0, 2)),
+    )
+
+
+def fits(ranks, x_in, proj, fout):
+    rows, width = proj.shape[3:]
+    return (
+        ranks == RANKS
+        and x_in.shape[1] == 4
+        and x_in.shape[2] == 2 * HEAD
+        and rows % 16 == 0
+        and rows <= 128
+        and width == HEADS * HEAD
+        and fout.shape[1] == 4 * rows
+    )
 
 
 def swapped(array, axis, stride):
@@ -132,6 +1425,19 @@
     vectors,
     cotangent,
 ):
+    if fits(lax.axis_size("dp"), x_in, proj_master, ffn_out_master):
+        return run_layer(
+            x_in,
+            lengths,
+            drops,
+            proj_master,
+            out_master,
+            ffn_in_master,
+            ffn_out_master,
+            join_master,
+            vectors,
+            cotangent,
+        )
     pages = x_in.shape[1]
     slots = x_in.shape[2]
     width = x_in.shape[3]

time: 1670 us -> 319 us (0.19)
  waiting for transfers between devices: 1320 us -> 0 us
  Pallas kernels: 0 us -> 315 us
  matrix products: 141 us -> 0 us
  local copies, waits for them, and re-layouts: 98.6 us -> 0 us
  blocking collectives: 41.3 us -> 0 us
  other arithmetic: 37.9 us -> 0 us
    reduce_scatter x4 -> x0, waiting for transfers between devices: 635 us -> none  [the longest x1 177 us: local(): lax.psum_scatter(grad_ffin[None], 'dp', scatter_dimension=1, tiled=True)]
    unnamed x13 -> x0, waiting for transfers between devices: 429 us -> none
    pallas_call x0 -> x2, Pallas kernels: none -> 315 us  [the longest x1 312 us: run_layer(): pl.pallas_call(partial(layer_kernel, rows), out_shape=[jax.ShapeDtypeStru...]
    all_gather x5 -> x0, waiting for transfers between devices: 254 us -> none  [the longest x1 103 us: local(): lax.all_gather(proj_master.astype(jnp.bfloat16), 'dp', axis=3, tiled=True)]
    dot_general x48 -> x0, matrix products: 141 us -> none  [the longest x12 54.8 us: product(): return jnp.dot(left, right, preferred_element_type=jnp.float32)]
    all_gather x1 -> x0, blocking collectives: 41.3 us -> none  [local(): lax.all_gather(vectors.astype(jnp.bfloat16), 'dp', axis=2, tiled=True)]
    unnamed x134 -> x0, local copies, waits for them, and re-layouts: 23.6 us -> none
    broadcast_in_dim x2 -> x0, local copies, waits for them, and re-layouts: 21.7 us -> none  [the longest x1 21.7 us: local(): grad_proj = jnp.stack([grad_proj_cross, grad_proj_self])[None]]
  transfers between devices with their start and end apart: 17 -> 0, of which waited for: 11 -> 0; matrix products, arithmetic and copies ran while one was open for 12% -> 0% of each run, Pallas kernels for 0% -> 0%
where the time goes in v1:
time: 319 us; the launch traced here: 316 us
  Pallas kernels  315 us (99%)
    pallas_call x1, Pallas kernels, run_layer(): pl.pallas_call(partial(layer_kernel, rows), out_shape=[jax.ShapeDtypeStru...  312 us

profile of v1, /device:TPU:0, one launch (start us, length us, event | category | flops | bytes accessed | tf_op | source)
XLA Modules:
  0.0 316.2 jit_solution(9915973539456687357)
XLA Ops:
  0.6 312.0 %shard_map.161 = (bf16[4,128,768]{2,1,0:T(8,128)(2,1)}, bf16[4,128,768]{2,1,0:T(8,128)(2,1)}, f32[6,48,768]{2,1,0:T(8,128)}, f32[2,48,768]{2,1,0:T(8,128)}, f32[...) custom-call(s32[4]{0:T(128)} %lengths.1, s32[4]{0:T(128)} %drops.1, ...), custom_call_target="tpu_custom_call" | custom-call | tf_op jit(solution)/shard_map/pallas_call | solution.py:1251
  312.6 3.3 %shard_map.162 = (bf16[4,128,768]{2,1,0:T(8,128)(2,1)}, bf16[4,128,768]{2,1,0:T(8,128)(2,1)}, f32[6,48,768]{2,1,0:T(8,128)}, f32[2,48,768]{2,1,0:T(8,128)}, f32[...) custom-call(bf16[4,128,768]{2,1,0:T(8,128)(2,1)} %get-tuple-element.24.refs_0_, ...), custom_call_target="tpu_custom_call" | custom-call | tf_op jit(solution)/shard_map/pallas_call | solution.py:1272

commit v2 on v1

--- a/solution.py
+++ b/solution.py
@@ -218,8 +218,8 @@
 
 
 class GatherByPlane:
-    def __init__(self, view, links):
-        self.view, self.k = view, links
+    def __init__(self, view, links, size):
+        self.view, self.k, self.size = view, links, size
         self.lines = [
             LineGather(partial(lambda q, z: view(z, q), q), links) for q in links.columns
         ]
@@ -233,8 +233,11 @@
         k = self.k
         for copy in self.sides:
             copy.wait_recv()
-        one, two = self.view(k.z, k.qx, 0, 1), self.view(k.z, k.qy, 1, 1)
-        self.corners = [k.send(one, one, k.y), k.send(two, two, k.x)]
+        one = self.view(k.z, k.qx, 0, 1)
+        self.corners = [k.send(one, one, k.y)]
+        if self.size == 2:
+            two = self.view(k.z, k.qy, 1, 1)
+            self.corners.append(k.send(two, two, k.x))
 
     def L(self, column):
         if column == 3:
@@ -638,7 +641,7 @@
     def fold(values):
         return jnp.sum(values.reshape(BLOCK // 8, 8, width), axis=0)
 
-    def norm_back(number, grad, after):
+    def norm_back(number, grad, after, run=None):
         part[...] = jnp.zeros_like(part)
 
         def step(at, i):
@@ -656,7 +659,7 @@
             grd[at] = result
             after(at, i, result)
 
-        by_rows(step)
+        (by_rows if run is None else run)(step)
         for i in range(2):
             vg[2 * number + i : 2 * number + i + 1, :] = jnp.sum(part[i], axis=0, keepdims=True)
 
@@ -748,8 +751,11 @@
 
     used = {}
 
-    def gather(item, by=GatherByLine):
-        return by(view(item), k)
+    def gather(item):
+        return GatherByLine(view(item), k)
+
+    def gather_by_plane(item):
+        return GatherByPlane(view(item), k, item[2])
 
     def keep_scatter(item):
         scatters.append(item)
@@ -831,7 +837,7 @@
     gQO = gather(ITEMS[2])
     gQK = gather(ITEMS[3])
     gVO = gather(ITEMS[4])
-    gJ = gather(ITEMS[5], GatherByPlane)
+    gJ = gather_by_plane(ITEMS[5])
     gvec = gather(VECTORS)
     sK = scatter(ITEMS[0])
     sV = scatter(ITEMS[1])
@@ -977,6 +983,14 @@
             at = pl.ds(first * BLOCK, (last - first) * BLOCK)
             swap((name, number), buffer.at[at], target.at[at], peer)
 
+    def theirs_in_two(name, result, target):
+        half = (count // BLOCK + 1) // 2 * BLOCK
+        for number, first, size in ((0, 0, half), (1, half, count - half)):
+            at = pl.ds(first, size)
+            acc[at] = result(pl.ds(count + first, size))
+            act[edge, at] = acc[at].astype(LOW)
+            swap((name, number), act.at[edge, at], target.at[at], k.x)
+
     def ln2():
         acc[...] = times(rows_in(o2)[...], weight(VO_SELF, 1))
 
@@ -1005,17 +1019,17 @@
         by_rows(step)
 
     def ffn_out_theirs():
-        acc[...] = times(mid[0, theirs], out_weight(0))
-        acc[...] += times(mid[1, theirs], out_weight(1))
-        narrow(acc, rows_in(edge))
-        swap(FFN, rows_in(edge), rows_in(back), k.x)
+        def rows_of_result(to):
+            return times(mid[0, to], out_weight(0)) + times(mid[1, to], out_weight(1))
+
+        theirs_in_two(FFN, rows_of_result, rows_in(back))
 
     def ffn_out_mine():
         for block in range(2):
             res[...] += times(mid[block, mine], out_weight(block))
 
     def ln3():
-        swapped(FFN)
+        swapped((FFN, 0), (FFN, 1))
 
         def step(at, i):
             del i
@@ -1057,12 +1071,13 @@
         logits = ea.at[mine]
         rows_in(edge)[...] = (grd[...] + times_transposed(logits[...], weight(JOIN, 1))).astype(LOW)
         swap("edge", rows_in(edge), rows_in(back))
-        square_grad(JOIN, 1, rows_in(far)[...], logits[...])
 
     def join_back_own():
         logits = ea.at[mine]
         res[...] += times_transposed(logits[...], weight(JOIN, 0))
-        square_grad(JOIN, 0, rows_in(state)[...], logits[...])
+
+    def join_grad(index):
+        square_grad(JOIN, index, rows_in(state + index)[...], rows_in(edge)[...])
 
     def keep_err(at, i, result):
         del i
@@ -1073,12 +1088,16 @@
 
     def ln3_back():
         swapped("edge")
-        norm_back(2, lambda at: res[at] + act[back, at].astype(FULL), keep_err)
-        swap(ERR, ea.at[mine], ea.at[theirs], k.x)
+
+        def grad(at):
+            act[edge, at] = ea[at]
+            return res[at] + act[back, at].astype(FULL)
+
+        norm_back(2, grad, keep_err, lambda step: in_two(step, ERR, ea, ea.at[theirs], k.x))
 
     def hidden_back(whose, block):
         if whose is theirs and block == 0:
-            swapped(ERR)
+            swapped((ERR, 0), (ERR, 1))
         first = 0 if whose is mine else count
         acc[...] = times_transposed(ea[whose], out_weight(block))
 
@@ -1096,10 +1115,11 @@
             pl.semaphore_signal(ready, inc=1, device_id=k.twin, device_id_type=MESH)
 
     def ffn_in_back_theirs():
-        acc[...] = times_transposed(slope[0, theirs], in_weight(0))
-        acc[...] += times_transposed(slope[1, theirs], in_weight(1))
-        narrow(acc, rows_in(edge))
-        swap(FFN_BACK, rows_in(edge), rows_in(far), k.x)
+        def rows_of_result(to):
+            one = times_transposed(slope[0, to], in_weight(0))
+            return one + times_transposed(slope[1, to], in_weight(1))
+
+        theirs_in_two(FFN_BACK, rows_of_result, rows_in(far))
 
     def ffn_in_back_mine():
         for block in range(2):
@@ -1111,7 +1131,7 @@
             fi[:, :, block, :, at] = grad.reshape(LINE, PLANE, rows, TILE)
 
     def ln2_back():
-        swapped(FFN_BACK)
+        swapped((FFN_BACK, 0), (FFN_BACK, 1))
         norm_back(1, lambda at: grd[at] + act[far, at].astype(FULL), keep_err)
         free(0)[...] = times_transposed(ea[mine], weight(VO_SELF, 1)).astype(LOW)
         square_grad(VO_SELF, 1, rows_in(o2)[...], ea[mine])
@@ -1145,25 +1165,24 @@
         narrow(grd, ea)
         pages_out(ea.at[mine], x_grad, 1)
 
-    start(); gV.L(); gvec.L(); cast1(); gJ.X(); gK.L(); gFO.X(); cast2(); gV.R(); gvec.R(); gQO.L(); gK.R(); gV.X()
-    gvec.X(); gK.X(); gQK.L(); gJ.C(); gVO.L(); gV.C(); gvec.C(); gK.C(); gQO.R(); gQO.X(); gK.F(); gFI.L(); kv0()
-    gV.F(); gvec.F(); vectors(); gQK.R(); gQK.X(); gQO.C(); gVO.R(); gFI.R(); gFO.L(0); gJ.L(2); kv1(); gVO.X()
-    gQO.F(); gQK.C(); gFO.L(1); gVO.C(); project_q1(); attend(0, 0, q1, k1, v1, o1); gFI.X(); gQK.F()
-    attend(1, 0, q1, k1, v1, o1); gJ.L(3); ln1(); project_self(q2, QK_SELF, 0); gFO.R(0); gVO.F()
-    project_self(k2, QK_SELF, 1); project_self(v2, VO_SELF, 0); attend(0, 1, q2, k2, v2, o2)
-    attend(1, 1, q2, k2, v2, o2); ln2(); gJ.L(1); gFO.R(1); gJ.L(0); gFI.F(); ffn_in(mine, 0); gJ.R(3)
-    ffn_in(mine, 1); ffn_in(theirs, 0); ffn_in(theirs, 1); gFO.F(); gJ.R(2); ffn_out_theirs(); ffn_out_mine()
-    gJ.R(0); gJ.R(1); ln3(); gJ.F(); join_own(); join_far(); gate(); join_back(); sJ1.C(); join_back_own()
-    ln3_back(); hidden_back(mine, 1); hidden_back(mine, 0); ffn_in_back_mine(); sJ1.X(); sJ0.C()
-    hidden_back(theirs, 0); hidden_back(theirs, 1); ffn_in_back_theirs(); sJ1.L(); out_grad(0); in_grad(1); sJ0.X()
-    sJ1.B(); in_grad(0); sFI.C(); out_grad(1); sFO.L(0); ln2_back(); sFO.L(1); attend_back(0, 1, q2, k2, v2)
-    sJ1.F(); attend_back(1, 1, q2, k2, v2); self_back(VO_SELF, 0, 2); sJ0.L(); sVO.C(); sFO.B(0)
-    self_back(QK_SELF, 0, 0); self_back(QK_SELF, 1, 1); sFI.L(); sQK.C(); ln1_back(); sFO.B(1)
-    attend_back(0, 0, q1, k1, v1); sVO.X(); sJ0.B(); sQK.X(); attend_back(1, 0, q1, k1, v1); sFI.B()
-    cross_query_back(); sQO.C(); svec.C(); sJ0.F(); sVO.L(); sQK.L(); cross_back(0); sQO.X(); svec.X(); sQK.B()
-    last_cross_back(); sVO.B(); sK.C(); sQO.L(); svec.L(); sFO.M(0); sV.C(); sQO.B(); svec.B(); sK.X(); sV.X()
-    sQK.F(); sFO.M(1); sFI.F(); sFO.X(); sK.L(); sV.L(); sK.B(); sFI.G(); sV.B(); sQO.F(); svec.F(); sFO.F(); sK.F()
-    sVO.F(); sV.F()
+    start(); cast1(); gV.L(); gvec.L(); gJ.X(); cast2(); gFO.X(); gQO.L(); gV.R(); gvec.R(); gJ.C(); gV.X()
+    gvec.X(); gQO.R(); gK.L(); gQK.L(); gK.R(); gV.C(); gvec.C(); gVO.L(); gQO.X(); gK.X(); gQK.R(); gFI.L()
+    gQO.C(); gQK.X(); gVO.R(); gK.C(); gFO.L(1); gVO.X(); gFI.R(); gK.F(); kv0(); gQO.F(); gFO.L(0); gV.F()
+    gvec.F(); vectors(); kv1(); gQK.C(); project_q1(); attend(0, 0, q1, k1, v1, o1); attend(1, 0, q1, k1, v1, o1)
+    gJ.L(3); ln1(); gVO.C(); gJ.L(2); gQK.F(); gFI.X(); gFO.R(1); project_self(q2, QK_SELF, 0)
+    project_self(k2, QK_SELF, 1); gJ.L(0); gVO.F(); project_self(v2, VO_SELF, 0); attend(0, 1, q2, k2, v2, o2)
+    attend(1, 1, q2, k2, v2, o2); ln2(); gFO.R(0); gJ.L(1); gFI.F(); ffn_in(theirs, 0); gFO.F(); ffn_in(theirs, 1)
+    ffn_out_theirs(); gJ.R(0); ffn_in(mine, 1); gJ.R(2); gJ.R(3); gJ.R(1); ffn_in(mine, 0); ffn_out_mine(); ln3()
+    gJ.F(); join_own(); join_far(); gate(); join_back(); join_back_own(); ln3_back(); join_grad(1)
+    hidden_back(mine, 1); join_grad(0); sJ1.C(); hidden_back(mine, 0); ffn_in_back_mine(); hidden_back(theirs, 0)
+    hidden_back(theirs, 1); sJ1.X(); ffn_in_back_theirs(); sJ0.C(); in_grad(0); in_grad(1); sFI.C(); sJ1.L()
+    out_grad(0); out_grad(1); sFO.L(0); sJ1.B(); ln2_back(); attend_back(0, 1, q2, k2, v2); sJ0.X(); sFO.B(0)
+    attend_back(1, 1, q2, k2, v2); self_back(VO_SELF, 0, 2); sVO.C(); sFI.L(); sJ0.L(); self_back(QK_SELF, 0, 0)
+    self_back(QK_SELF, 1, 1); sJ1.F(); sVO.X(); sQK.C(); ln1_back(); sFO.L(1); attend_back(0, 0, q1, k1, v1)
+    sJ0.B(); sFI.B(); attend_back(1, 0, q1, k1, v1); sVO.L(); sQK.X(); cross_query_back(); sFO.B(1); cross_back(0)
+    sQO.C(); svec.C(); sFO.M(0); sQO.X(); svec.X(); sVO.B(); sK.C(); last_cross_back(); sFI.F(); sFO.M(1); sJ0.F()
+    sQK.L(); sQK.B(); sK.X(); sV.C(); sQO.L(); svec.L(); sFI.G(); sQO.B(); svec.B(); sVO.F(); sV.X(); sK.L()
+    sQK.F(); sFO.X(); sV.L(); sV.B(); sQO.F(); svec.F(); sK.B(); sV.F(); sFO.F(); sK.F()
     for copy in page_copies:
         copy.wait()
     for item in scatters:

time: 319 us -> 321 us (level)
  no operation moved by 1% of the time
where the time goes in v2:
time: 321 us; the launch traced here: 318 us
  Pallas kernels  317 us (99%)
    pallas_call x1, Pallas kernels, run_layer(): pl.pallas_call(partial(layer_kernel, rows), out_shape=[jax.ShapeDtypeStru...  314 us

profile of v2, /device:TPU:0, one launch (start us, length us, event | category | flops | bytes accessed | tf_op | source)
XLA Modules:
  0.0 318.2 jit_solution(2922664501111815763)
XLA Ops:
  0.6 314.0 %shard_map.161 = (bf16[4,128,768]{2,1,0:T(8,128)(2,1)}, bf16[4,128,768]{2,1,0:T(8,128)(2,1)}, f32[6,48,768]{2,1,0:T(8,128)}, f32[2,48,768]{2,1,0:T(8,128)}, f32[...) custom-call(s32[4]{0:T(128)} %lengths.1, s32[4]{0:T(128)} %drops.1, ...), custom_call_target="tpu_custom_call" | custom-call | tf_op jit(solution)/shard_map/pallas_call | solution.py:1270
  314.6 3.3 %shard_map.162 = (bf16[4,128,768]{2,1,0:T(8,128)(2,1)}, bf16[4,128,768]{2,1,0:T(8,128)(2,1)}, f32[6,48,768]{2,1,0:T(8,128)}, f32[2,48,768]{2,1,0:T(8,128)}, f32[...) custom-call(bf16[4,128,768]{2,1,0:T(8,128)(2,1)} %get-tuple-element.24.refs_0_, ...), custom_call_target="tpu_custom_call" | custom-call | tf_op jit(solution)/shard_map/pallas_call | solution.py:1291

commit v3 on v2

--- a/solution.py
+++ b/solution.py
@@ -35,7 +35,7 @@
 VECTORS = None
 H2, FFN, STATE, ERR, FFN_BACK = range(5)
 CORNER_RING, SIDE_RING, LINE_RING, HOP_RING, PAIR_RING = 3, 4, 5, 5, 3
-BLOCK = 64
+BLOCK = 112
 KEPT = 112
 TILE = 256
 TILES = tuple(pl.ds(at, TILE) for at in range(0, 768, TILE))
@@ -673,7 +673,7 @@
         return jnp.where(first, values[:KEPT], values[KEPT:])
 
     def by_heads(half, body):
-        group = 3
+        group = 6
 
         def step(i):
             page = i // (pairs // group)
@@ -1165,24 +1165,24 @@
         narrow(grd, ea)
         pages_out(ea.at[mine], x_grad, 1)
 
-    start(); cast1(); gV.L(); gvec.L(); gJ.X(); cast2(); gFO.X(); gQO.L(); gV.R(); gvec.R(); gJ.C(); gV.X()
-    gvec.X(); gQO.R(); gK.L(); gQK.L(); gK.R(); gV.C(); gvec.C(); gVO.L(); gQO.X(); gK.X(); gQK.R(); gFI.L()
-    gQO.C(); gQK.X(); gVO.R(); gK.C(); gFO.L(1); gVO.X(); gFI.R(); gK.F(); kv0(); gQO.F(); gFO.L(0); gV.F()
-    gvec.F(); vectors(); kv1(); gQK.C(); project_q1(); attend(0, 0, q1, k1, v1, o1); attend(1, 0, q1, k1, v1, o1)
-    gJ.L(3); ln1(); gVO.C(); gJ.L(2); gQK.F(); gFI.X(); gFO.R(1); project_self(q2, QK_SELF, 0)
-    project_self(k2, QK_SELF, 1); gJ.L(0); gVO.F(); project_self(v2, VO_SELF, 0); attend(0, 1, q2, k2, v2, o2)
-    attend(1, 1, q2, k2, v2, o2); ln2(); gFO.R(0); gJ.L(1); gFI.F(); ffn_in(theirs, 0); gFO.F(); ffn_in(theirs, 1)
-    ffn_out_theirs(); gJ.R(0); ffn_in(mine, 1); gJ.R(2); gJ.R(3); gJ.R(1); ffn_in(mine, 0); ffn_out_mine(); ln3()
-    gJ.F(); join_own(); join_far(); gate(); join_back(); join_back_own(); ln3_back(); join_grad(1)
-    hidden_back(mine, 1); join_grad(0); sJ1.C(); hidden_back(mine, 0); ffn_in_back_mine(); hidden_back(theirs, 0)
-    hidden_back(theirs, 1); sJ1.X(); ffn_in_back_theirs(); sJ0.C(); in_grad(0); in_grad(1); sFI.C(); sJ1.L()
-    out_grad(0); out_grad(1); sFO.L(0); sJ1.B(); ln2_back(); attend_back(0, 1, q2, k2, v2); sJ0.X(); sFO.B(0)
-    attend_back(1, 1, q2, k2, v2); self_back(VO_SELF, 0, 2); sVO.C(); sFI.L(); sJ0.L(); self_back(QK_SELF, 0, 0)
-    self_back(QK_SELF, 1, 1); sJ1.F(); sVO.X(); sQK.C(); ln1_back(); sFO.L(1); attend_back(0, 0, q1, k1, v1)
-    sJ0.B(); sFI.B(); attend_back(1, 0, q1, k1, v1); sVO.L(); sQK.X(); cross_query_back(); sFO.B(1); cross_back(0)
-    sQO.C(); svec.C(); sFO.M(0); sQO.X(); svec.X(); sVO.B(); sK.C(); last_cross_back(); sFI.F(); sFO.M(1); sJ0.F()
-    sQK.L(); sQK.B(); sK.X(); sV.C(); sQO.L(); svec.L(); sFI.G(); sQO.B(); svec.B(); sVO.F(); sV.X(); sK.L()
-    sQK.F(); sFO.X(); sV.L(); sV.B(); sQO.F(); svec.F(); sK.B(); sV.F(); sFO.F(); sK.F()
+    start(); gV.L(); gvec.L(); cast1(); gFO.X(); cast2(); gQO.L(); gJ.X(); gV.R(); gvec.R(); gV.X(); gvec.X()
+    gQO.R(); gK.L(); gQK.L(); gJ.C(); gQO.X(); gV.C(); gvec.C(); gK.R(); gQK.R(); gVO.L(); gK.X(); gFI.L(); gQO.C()
+    gQK.X(); gFO.L(0); gVO.R(); gK.C(); gVO.X(); gFI.R(); gFO.L(1); gQO.F(); gK.F(); kv0(); gV.F(); gvec.F()
+    vectors(); kv1(); gQK.C(); project_q1(); attend(0, 0, q1, k1, v1, o1); gVO.C(); attend(1, 0, q1, k1, v1, o1)
+    ln1(); gQK.F(); project_self(q2, QK_SELF, 0); gFI.X(); gJ.L(0); project_self(k2, QK_SELF, 1); gVO.F()
+    project_self(v2, VO_SELF, 0); gFO.R(0); attend(0, 1, q2, k2, v2, o2); attend(1, 1, q2, k2, v2, o2); ln2()
+    gJ.L(1); gFO.R(1); gJ.L(3); gFI.F(); gJ.L(2); ffn_in(theirs, 0); gFO.F(); ffn_in(theirs, 1); ffn_out_theirs()
+    gJ.R(0); ffn_in(mine, 0); gJ.R(1); gJ.R(3); ffn_in(mine, 1); ffn_out_mine(); gJ.R(2); ln3(); gJ.F(); join_own()
+    join_far(); gate(); join_back(); join_back_own(); ln3_back(); hidden_back(mine, 1); hidden_back(mine, 0)
+    join_grad(1); ffn_in_back_mine(); sJ1.C(); join_grad(0); sJ0.C(); hidden_back(theirs, 0); sJ1.X()
+    hidden_back(theirs, 1); ffn_in_back_theirs(); in_grad(1); in_grad(0); sFI.C(); sJ1.L(); out_grad(0); sJ1.B()
+    out_grad(1); sFO.L(0); ln2_back(); attend_back(0, 1, q2, k2, v2); sFO.B(0); sJ0.X()
+    attend_back(1, 1, q2, k2, v2); sJ1.F(); sFI.L(); self_back(VO_SELF, 0, 2); sVO.C(); self_back(QK_SELF, 0, 0)
+    sJ0.L(); self_back(QK_SELF, 1, 1); sQK.C(); sFI.B(); ln1_back(); sVO.X(); sFO.L(1)
+    attend_back(0, 0, q1, k1, v1); sQK.X(); sJ0.B(); attend_back(1, 0, q1, k1, v1); cross_query_back(); sVO.L()
+    sQO.C(); svec.C(); sJ0.F(); sFO.B(1); cross_back(0); sVO.B(); sQO.X(); svec.X(); last_cross_back(); sK.C()
+    sQK.L(); sFO.M(1); sQK.B(); sK.X(); sV.C(); sQO.L(); svec.L(); sK.L(); sFO.M(0); sV.X(); sQO.B(); svec.B()
+    sQK.F(); sFO.X(); sFI.F(); sK.B(); sV.L(); sV.B(); sFI.G(); sK.F(); sVO.F(); sQO.F(); svec.F(); sFO.F(); sV.F()
     for copy in page_copies:
         copy.wait()
     for item in scatters:

time: 321 us -> 316 us (0.984)
  Pallas kernels: 317 us -> 312 us
    pallas_call x1, Pallas kernels: 314 us -> 309 us  [run_layer(): pl.pallas_call(partial(layer_kernel, rows), out_shape=[jax.ShapeDtypeStru...]
where the time goes in v3:
time: 316 us; the launch traced here: 313 us
  Pallas kernels  312 us (99%)
    pallas_call x1, Pallas kernels, run_layer(): pl.pallas_call(partial(layer_kernel, rows), out_shape=[jax.ShapeDtypeStru...  309 us

profile of v3, /device:TPU:0, one launch (start us, length us, event | category | flops | bytes accessed | tf_op | source)
XLA Modules:
  0.0 312.9 jit_solution(12596961273418657663)
XLA Ops:
  0.6 308.7 %shard_map.161 = (bf16[4,128,768]{2,1,0:T(8,128)(2,1)}, bf16[4,128,768]{2,1,0:T(8,128)(2,1)}, f32[6,48,768]{2,1,0:T(8,128)}, f32[2,48,768]{2,1,0:T(8,128)}, f32[...) custom-call(s32[4]{0:T(128)} %lengths.1, s32[4]{0:T(128)} %drops.1, ...), custom_call_target="tpu_custom_call" | custom-call | tf_op jit(solution)/shard_map/pallas_call | solution.py:1270
  309.3 3.3 %shard_map.162 = (bf16[4,128,768]{2,1,0:T(8,128)(2,1)}, bf16[4,128,768]{2,1,0:T(8,128)(2,1)}, f32[6,48,768]{2,1,0:T(8,128)}, f32[2,48,768]{2,1,0:T(8,128)}, f32[...) custom-call(bf16[4,128,768]{2,1,0:T(8,128)(2,1)} %get-tuple-element.24.refs_0_, ...), custom_call_target="tpu_custom_call" | custom-call | tf_op jit(solution)/shard_map/pallas_call | solution.py:1291

commit v4 on v3

--- a/solution.py
+++ b/solution.py
@@ -35,7 +35,7 @@
 VECTORS = None
 H2, FFN, STATE, ERR, FFN_BACK = range(5)
 CORNER_RING, SIDE_RING, LINE_RING, HOP_RING, PAIR_RING = 3, 4, 5, 5, 3
-BLOCK = 112
+BLOCK = 64
 KEPT = 112
 TILE = 256
 TILES = tuple(pl.ds(at, TILE) for at in range(0, 768, TILE))

time: 316 us -> 316 us (level)
  no operation moved by 1% of the time
where the time goes in v4:
time: 316 us; the launch traced here: 313 us
  Pallas kernels  312 us (99%)
    pallas_call x1, Pallas kernels, run_layer(): pl.pallas_call(partial(layer_kernel, rows), out_shape=[jax.ShapeDtypeStru...  309 us

profile of v4, /device:TPU:0, one launch (start us, length us, event | category | flops | bytes accessed | tf_op | source)
XLA Modules:
  0.0 313.3 jit_solution(7166882665566230016)
XLA Ops:
  0.6 309.1 %shard_map.161 = (bf16[4,128,768]{2,1,0:T(8,128)(2,1)}, bf16[4,128,768]{2,1,0:T(8,128)(2,1)}, f32[6,48,768]{2,1,0:T(8,128)}, f32[2,48,768]{2,1,0:T(8,128)}, f32[...) custom-call(s32[4]{0:T(128)} %lengths.1, s32[4]{0:T(128)} %drops.1, ...), custom_call_target="tpu_custom_call" | custom-call | tf_op jit(solution)/shard_map/pallas_call | solution.py:1270
  309.7 3.3 %shard_map.162 = (bf16[4,128,768]{2,1,0:T(8,128)(2,1)}, bf16[4,128,768]{2,1,0:T(8,128)(2,1)}, f32[6,48,768]{2,1,0:T(8,128)}, f32[2,48,768]{2,1,0:T(8,128)}, f32[...) custom-call(bf16[4,128,768]{2,1,0:T(8,128)(2,1)} %get-tuple-element.24.refs_0_, ...), custom_call_target="tpu_custom_call" | custom-call | tf_op jit(solution)/shard_map/pallas_call | solution.py:1291
